TPU v7x, 32 devices: a whole 2x2x4 slice. The times are simulated.
32 devices in a mesh: groups: 2 (over x), seq: 8 (over z, y), tp: 2 (over core).
Axes of the slice: x: 2, y: 2, z: 4, core: 2. Of those that a mesh axis runs over, the one named last changes fastest.
Arguments:
- queries: bfloat16 [16384, 4096], P(('groups', 'seq'), 'tp'), parts along dimension 0, may hold values from -6 to 6
- keys: bfloat16 [16384, 4096], P(('groups', 'seq'), 'tp'), parts along dimension 0, may hold values from -6 to 6
- values: bfloat16 [16384, 4096], P(('groups', 'seq'), 'tp'), parts along dimension 0, may hold values from -6 to 6
- log_decay: float32 [16384, 32], P(('groups', 'seq'), 'tp'), parts along dimension 0, may hold values from -1 to 0, as said below
- gate: bfloat16 [16384, 4096], P(('groups', 'seq'), 'tp'), parts along dimension 0, may hold values from -6 to 6
- gain: bfloat16 [4096], P('tp'), may hold values from 0.099609375 to 1.8984375
- doc_lengths: int32 [16], P('groups'), parts along dimension 0, may hold values from 1 to 4096, 8192 in all
- owner_ids: int32 [16], P('groups'), parts along dimension 0, may hold values from 0 to 7, each once
Outputs:
- mixed: bfloat16 [16384, 4096], P(('groups', 'seq'), 'tp'), parts along dimension 0
- owner_states: bfloat16 [16, 32, 128, 128], P(('groups', 'seq'), 'tp'), parts along dimension 0
There are 2 independent parts, one for each index of `groups`. A program takes and returns all parts, laid end to end along the dimension named above; an argument that names none is the same for every part. Nothing has to cross between parts.
Inputs may be any that keep to these rules, and one draw needn't show every extreme that they name: `doc_lengths`: positive lengths summing to 8192; the longest prompt has exactly 4096 tokens. `owner_ids`: a permutation of the owner slots. `log_decay`: negative.
All inputs are finite; a program needn't handle non-finite values.
Results may differ from a plain program's by a relative error of at most 0.0049.
Values may be sent and summed in bfloat16 or wider, within the bound.
No kernel may reach another device: no remote copies, remote signals or barrier semaphores. Data moves between devices by JAX's collectives and lax.ppermute only.
A program may use at most 192 MiB of HBM per device.

v0:
```python
import functools
import math

import jax
import jax.numpy as jnp
from jax import lax
from jax.experimental import pallas as pl
from jax.experimental.pallas import tpu as pltpu
from jax.sharding import PartitionSpec as P

BLK = 512
SIDE = 3
SENT = (2, 1)
EXTRA = 16
CHUNK = 256
MEMBERS = 4
TILE = 256
EARLY = (4, 4)
NEG = -1e30
LOG2E = math.log2(math.e)
SCALE = 128**-0.5
F32, BF16 = jnp.float32, jnp.bfloat16
SMEM = pl.BlockSpec(memory_space=pltpu.SMEM)
VMEM = pl.BlockSpec(memory_space=pltpu.VMEM)
LIMIT = pltpu.CompilerParams(vmem_limit_bytes=60 * 2**20)
SMALL = pltpu.CompilerParams(vmem_limit_bytes=48 * 2**20)


def dot(a, b, contract=((1,), (0,))):
    return lax.dot_general(a, b, (contract, ((), ())), preferred_element_type=F32)


def iota(shape, dim):
    return lax.broadcasted_iota(jnp.int32, shape, dim)


def read_ends(len_ref, count):
    ends, total = [], jnp.int32(0)
    for d in range(count):
        total = total + len_ref[d]
        ends.append(total)
    return ends


def run_end(ends, pos):
    best = ends[-1]
    for e in reversed(ends[:-1]):
        best = jnp.where(e > pos, e, best)
    return best


def run_start(ends, pos):
    best = jnp.zeros_like(pos)
    for e in ends[:-1]:
        best = jnp.where(e <= pos, e, best)
    return best


def split3(x):
    hi = x.astype(BF16)
    rest = x - hi.astype(F32)
    mid = rest.astype(BF16)
    return hi, mid, (rest - mid.astype(F32)).astype(BF16)


def cum_rows(ld_ref, crow_ref):
    heads, rows = ld_ref.shape
    upper = (iota((BLK, BLK), 0) <= iota((BLK, BLK), 1)).astype(F32).astype(BF16)
    base = jnp.zeros((heads, 1), F32)
    for b in range(rows // BLK):
        part = ld_ref[:, b * BLK : (b + 1) * BLK] * LOG2E
        sums = dot(jnp.concatenate(split3(part), axis=0), upper)
        row = sums[2 * heads :] + sums[heads : 2 * heads] + sums[:heads] + base
        crow_ref[:, b * BLK : (b + 1) * BLK] = row
        base = row[:, BLK - 1 :]


def value_at(cum, at, index):
    return jnp.sum(jnp.where(at == index, cum, 0.0), axis=1, keepdims=True)


def span_weights(cum, at, low, high):
    inside = (at >= low) & (at <= high)
    return jnp.exp2(jnp.where(inside, value_at(cum, at, high) - cum, NEG) + math.log2(SCALE))


def weigh(flipped, w_ref, h):
    weights = [jnp.broadcast_to(w_ref[pl.ds(h + j, 1), :], (128, flipped.shape[1])) for j in range(2)]
    return (flipped.astype(F32) * jnp.concatenate(weights, axis=0)).astype(BF16)


def whole(shape):
    return pl.BlockSpec(shape, lambda j: (0,) * len(shape))


def pieces_kernel(by_owner, len_ref, own_ref, ld_ref, k_ref, v_ref, *refs):
    if by_owner:
        side_ref, crow_ref, w_ref, keep_ref = refs
        slots = keep_ref.shape[0]
    else:
        side_refs, crow_ref, flag_ref = refs[:2], refs[2], refs[3]
        last_refs = refs[4 : 4 + MEMBERS]
        w_ref, first_ref, high_ref, weighted_ref, prefix_ref = refs[4 + MEMBERS :]
        slots = SIDE
    heads, rows = crow_ref.shape
    step = pl.program_id(0)
    hp = v_ref.shape[1] // 128
    me = lax.axis_index("seq")

    @pl.when(step == 0)
    def _():
        cum_rows(ld_ref, crow_ref)
        first = me * rows
        last = first + rows - 1
        ends = read_ends(len_ref, len_ref.shape[0])
        starts = [jnp.int32(0)] + ends[:-1]
        lows = [jnp.int32(0)] * slots
        highs = [jnp.int32(-1)] * slots
        place, rank, previous = jnp.int32(0), jnp.int32(0), jnp.int32(-1)
        crowded, owned_in, owned_late = jnp.int32(0), jnp.int32(0), jnp.int32(0)
        for d in range(len(ends)):
            here = (ends[d] > first) & (ends[d] <= last)
            low = jnp.maximum(starts[d] - first, 0)
            for s in range(slots):
                mine = here & ((place >= SIDE) & (own_ref[d] == s) if by_owner else (place == s))
                lows[s] = jnp.where(mine, low, lows[s])
                highs[s] = jnp.where(mine, ends[d] - 1 - first, highs[s])
            place = place + here.astype(jnp.int32)
            device = (ends[d] - 1) // rows
            rank = jnp.where(device == previous, rank + 1, 0)
            previous = device
            late = ((rank >= SIDE) & (ends[d] != (device + 1) * rows)).astype(jnp.int32)
            crowded = jnp.maximum(crowded, late)
            owned_in = jnp.where(own_ref[d] == me, device, owned_in)
            owned_late = jnp.where(own_ref[d] == me, late, owned_late)
        at = iota((heads, rows), 1)
        cum = crow_ref[...]
        total = jnp.zeros((heads, rows), F32)
        for s in range(slots):
            total = total + span_weights(cum, at, lows[s], highs[s])
        if by_owner:
            row_at = iota((16, rows), 1)
            for s in range(slots):
                inside = (row_at >= lows[s]) & (row_at <= highs[s])
                keep_ref[s] = jnp.where(inside, 1.0, 0.0).astype(BF16)
        else:
            total = total + span_weights(cum, at, jnp.maximum(run_start(ends, last) - first, 0), rows - 1)
            flag_ref[0] = owned_in // MEMBERS
            flag_ref[1] = owned_late
            flag_ref[2] = crowded
            flag_ref[3] = owned_in
            high = jnp.int32(-1)
            for s in range(slots):
                high = jnp.maximum(high, highs[s])
                high_ref[s] = high
            stop = jnp.minimum(run_end(ends, first) - 1 - first, rows - 1)
            goes_on = (run_start(ends, first) < first).astype(F32)
            first_ref[...] = jnp.broadcast_to(jnp.exp2(value_at(cum, at, stop)) * goes_on, (heads, 128))
        w_ref[...] = total

    def own(states, j):
        return states[j * 128 : (j + 1) * 128, j * 128 : (j + 1) * 128]

    if by_owner:
        weighted = weigh(k_ref[...].T, w_ref, step * hp).reshape(16, 16, rows)
        for s in range(slots):
            states = dot((weighted * keep_ref[s][None]).reshape(256, rows), v_ref[...])
            for j in range(2):
                side_ref[s, j] = own(states, j).astype(BF16)
        return

    pairs = range(0, hp, 2)
    lanes = {i: slice(i * 128, (i + 2) * 128) for i in pairs}
    for i in pairs:
        weighted_ref[lanes[i], :] = weigh(k_ref[:, lanes[i]].T, w_ref, step * hp + i)
    totals = {}
    for i in pairs:
        sums = [jnp.zeros((128, 128), F32)] * 2
        for t in range(rows // TILE):
            span = slice(t * TILE, (t + 1) * TILE)
            states = dot(weighted_ref[lanes[i], span], v_ref[span, lanes[i]])
            for j in range(2):
                prefix_ref[t, i + j] = sums[j]
                sums[j] = sums[j] + own(states, j)
        totals[i] = sums
    ended = {i: [jnp.zeros((128, 128), F32)] * 2 for i in pairs}
    for s in range(slots):
        high = high_ref[s]
        tile = jnp.maximum(high, 0) // TILE
        start = pl.multiple_of(tile * TILE, TILE)
        keep = jnp.where(start + iota((16, TILE), 1) <= high, 1.0, 0.0).astype(BF16)
        part, slot = (0, s) if s < SENT[0] else (1, s - SENT[0])
        for i in pairs:
            kept = weighted_ref[lanes[i], pl.ds(start, TILE)].reshape(16, 16, TILE) * keep[None]
            states = dot(kept.reshape(256, TILE), v_ref[pl.ds(start, TILE), lanes[i]])
            for j in range(2):
                until = own(states, j) + prefix_ref[tile, i + j]
                at = (slot * hp + i + j) * 128
                side_refs[part][0, at : at + 128, :] = (until - ended[i][j]).astype(BF16)
                ended[i][j] = until
    rate = first_ref[pl.ds(step * hp, hp), :]
    high = rate.astype(BF16).astype(F32)
    pad = jnp.zeros((EXTRA - 2 * hp, 128), F32)
    tail = jnp.concatenate([high, rate - high, pad], axis=0).astype(BF16)
    last_states = [(totals[i][j] - ended[i][j]).astype(BF16) for i in pairs for j in range(2)]
    for x, last_ref in enumerate(last_refs):

        @pl.when((step ^ (me % MEMBERS)) == x)
        def _():
            for i in range(hp):
                last_ref[i * 128 : (i + 1) * 128, :] = last_states[i]
            last_ref[hp * 128 :, :] = tail


def piece_states(doc_lengths, owner_ids, decay_rows, keys, values, spread=0):
    heads, rows = decay_rows.shape
    by_owner = spread > 0
    hp = 2 if by_owner else heads // MEMBERS
    wide = pl.BlockSpec((rows, hp * 128), lambda j: (0, j))
    scratch = [pltpu.VMEM((heads, rows), F32)]
    if by_owner:
        shapes = [jax.ShapeDtypeStruct((spread, heads, 128, 128), BF16), jax.ShapeDtypeStruct((heads, rows), F32)]
        specs = [pl.BlockSpec((spread, hp, 128, 128), lambda j: (0, j, 0, 0)), whole((heads, rows))]
        scratch.append(pltpu.VMEM((spread, 16, rows), BF16))
    else:
        last = (hp * 128 + EXTRA, 128)
        shapes = [
            *[jax.ShapeDtypeStruct((MEMBERS, n * hp * 128, 128), BF16) for n in SENT],
            jax.ShapeDtypeStruct((heads, rows), F32),
            jax.ShapeDtypeStruct((4,), jnp.int32),
            *[jax.ShapeDtypeStruct(last, BF16)] * MEMBERS,
        ]
        specs = [pl.BlockSpec((1, n * hp * 128, 128), lambda j: (j, 0, 0)) for n in SENT]
        specs += [whole((heads, rows)), SMEM] + [whole(last)] * MEMBERS
        scratch += [
            pltpu.VMEM((heads, 128), F32),
            pltpu.SMEM((SIDE,), jnp.int32),
            pltpu.VMEM((hp * 128, rows), BF16),
            pltpu.VMEM((rows // TILE, hp, 128, 128), F32),
        ]
    return pl.pallas_call(
        functools.partial(pieces_kernel, by_owner),
        grid=(heads // hp,),
        in_specs=[SMEM, SMEM, whole((heads, rows)), wide, wide],
        out_specs=specs,
        out_shape=shapes,
        scratch_shapes=scratch,
        compiler_params=LIMIT,
        cost_estimate=pl.CostEstimate(
            flops=2 * heads * rows * 128 * 256, bytes_accessed=rows * heads * 128 * 4, transcendentals=heads * rows
        ),
        name="piece_states",
    )(doc_lengths, owner_ids, decay_rows, keys, values)


def head_column(ccol_ref, h):
    cols = ccol_ref[...]
    return jnp.sum(jnp.where(iota(cols.shape, 1) == h, cols, 0.0), axis=1, keepdims=True)


def fill_columns(crow_ref, ccol_ref):
    heads, rows = crow_ref.shape
    for r0 in range(0, rows, 128):
        part = crow_ref[:, r0 : r0 + 128]
        part = jnp.concatenate([part, jnp.zeros((128 - heads, 128), F32)], axis=0)
        ccol_ref[r0 : r0 + 128, :] = part.T


def fill_bias(first, ends, bias_ref):
    for c in range(bias_ref.shape[0] // CHUNK):
        base = first + c * CHUNK
        t_pos = base + iota((CHUNK, 1), 0)
        start = run_start(ends, t_pos)
        s_pos = base + iota((CHUNK, CHUNK), 1)
        keep = (s_pos <= t_pos) & (s_pos >= start)
        bias_ref[c * CHUNK : (c + 1) * CHUNK, :] = jnp.where(keep, math.log2(SCALE), NEG)


def attend(first, ends, q_ref, k_ref, v_ref, h, crow_ref, ccol_ref, bias_ref, states, emit):
    rows = q_ref.shape[0]
    pair = range(2)
    half = CHUNK // 2
    lanes = [slice(i * 128, (i + 1) * 128) for i in pair]
    row_all = [crow_ref[pl.ds(h + i, 1), :] for i in pair]
    col_all = [head_column(ccol_ref, h + i) for i in pair]
    starts = range(0, rows, CHUNK)
    spans = [slice(r0, r0 + CHUNK) for r0 in starts]
    reach = [run_end(ends, first + r0 - 1) - (first + r0) for r0 in starts]
    base = [[row_all[i][:, r0 - 1 : r0] if r0 else jnp.zeros((1, 1), F32) for r0 in starts] for i in pair]

    fresh = [[], []]
    for c, r0 in enumerate(starts[:-1]):
        since = run_start(ends, first + r0 + CHUNK - 1) - (first + r0)
        inside = iota((1, CHUNK), 1) >= since
        for i in pair:
            row = row_all[i][:, spans[c]]
            weight = jnp.exp2(jnp.where(inside, row[:, CHUNK - 1 :] - row, NEG) + math.log2(SCALE))
            flipped = k_ref[spans[c], lanes[i]].T
            fresh[i].append(dot((flipped.astype(F32) * weight).astype(BF16), v_ref[spans[c], lanes[i]]))
    carried = []
    for i in pair:
        state = None if states is None else states[i]
        chain = [None if state is None else state.astype(BF16)]
        for c in range(len(starts) - 1):
            if state is None:
                state = fresh[i][c]
            else:
                total = row_all[i][:, starts[c] + CHUNK - 1 : starts[c] + CHUNK]
                state = fresh[i][c] + state * jnp.exp2(jnp.where(CHUNK <= reach[c], total - base[i][c], NEG))
            chain.append(state.astype(BF16))
        carried.append(chain)

    def products(c):
        result = []
        for i in pair:
            query = q_ref[spans[c], lanes[i]]
            scores = dot(query, k_ref[spans[c], lanes[i]], ((1,), (1,)))
            result.append((scores, None if carried[i][c] is None else dot(query, carried[i][c])))
        return result

    ahead = products(0)
    for c, r0 in enumerate(starts):
        current = ahead
        if c + 1 < len(starts):
            ahead = products(c + 1)
        for part in range(2):
            t0, width = part * half, (part + 1) * half
            rows_here = slice(r0 + t0, r0 + t0 + half)
            for i in pair:
                scores, carry = current[i]
                col = col_all[i][rows_here]
                decay = jnp.exp2((col - row_all[i][:, r0 : r0 + width]) + bias_ref[rows_here, :width])
                weights = (scores[t0 : t0 + half, :width] * decay).astype(BF16)
                att = dot(weights, v_ref[r0 : r0 + width, lanes[i]])
                if carry is not None:
                    lead = jnp.exp2(jnp.where(t0 + iota((half, 1), 0) < reach[c], col - base[i][c], NEG))
                    att = att + lead * carry[t0 : t0 + half]
                emit(lanes[i], r0 + t0, half, att)


def early_kernel(pairs_before, len_ref, q_ref, k_ref, v_ref, crow_ref, *refs):
    out_ref, bias_ref, ccol_ref = refs[-3:]
    rows = q_ref.shape[0]
    step = pl.program_id(0)
    first = lax.axis_index("seq") * rows
    ends = read_ends(len_ref, len_ref.shape[0])

    @pl.when(step == 0)
    def _():
        fill_bias(first, ends, bias_ref)
        fill_columns(crow_ref, ccol_ref)

    def emit(lanes, t0, size, att):
        out_ref[t0 : t0 + size, lanes] = att

    attend(first, ends, q_ref, k_ref, v_ref, (step + pairs_before) * 2, crow_ref, ccol_ref, bias_ref, None, emit)


def early_attention(doc_lengths, queries, keys, values, crow, before, part):
    heads, rows = crow.shape
    skip = sum(EARLY[:part]) // 2
    wide = pl.BlockSpec((rows, 256), lambda j: (0, j + skip))
    count = EARLY[part]
    return pl.pallas_call(
        functools.partial(early_kernel, skip),
        grid=(count // 2,),
        in_specs=[SMEM, wide, wide, wide, whole((heads, rows))] + [pl.BlockSpec(memory_space=pl.ANY)] * len(before),
        out_specs=wide,
        out_shape=jax.ShapeDtypeStruct((rows, sum(EARLY) * 128), F32),
        input_output_aliases={5: 0} if before else {},
        scratch_shapes=[pltpu.VMEM((rows, CHUNK), F32), pltpu.VMEM((rows, 128), F32)],
        compiler_params=LIMIT,
        cost_estimate=pl.CostEstimate(
            flops=count * rows * CHUNK * 128 * 8, bytes_accessed=rows * count * 128 * 10, transcendentals=count * rows * CHUNK
        ),
        name="early_attention",
    )(doc_lengths, queries, keys, values, crow, *before)


def gather_last(refs, last_ref):
    me = lax.axis_index("seq") % MEMBERS
    for x, ref in enumerate(refs):
        last_ref[me ^ x] = ref[...]


def decay_of(last_ref, e, i, hp):
    extra = last_ref[e, hp * 128 :, :].astype(F32)
    return extra[i : i + 1, :] + extra[hp + i : hp + i + 1, :]


def scan_quad(rows, len_ref, last_ref, state, i, hp, note):
    members = last_ref.shape[0]
    ends = read_ends(len_ref, len_ref.shape[0])
    base = lax.axis_index("seq") // members * members
    for e in range(members):
        note(e, state)
        low = (base + e) * rows
        inner = jnp.int32(0)
        for end in ends:
            inner = inner + ((end > low) & (end < low + rows)).astype(jnp.int32)
        passes = (inner == 0).astype(F32)
        piece = last_ref[e, i * 128 : (i + 1) * 128, :].astype(F32)
        state = state * (decay_of(last_ref, e, i, hp) * passes) + piece
    return state


def leave_kernel(rows, len_ref, *refs):
    out_ref, last_ref = refs[-2:]
    gather_last(refs[:MEMBERS], last_ref)
    hp = out_ref.shape[0]
    for i in range(hp):
        state = jnp.zeros((128, 128), F32)
        if len(refs) > MEMBERS + 2:
            state = refs[MEMBERS][i].astype(F32)
        state = scan_quad(rows, len_ref, last_ref, state, i, hp, lambda e, x: None)
        out_ref[i] = state.astype(BF16)


def leave_quad(doc_lengths, last, coming, rows, hp):
    return pl.pallas_call(
        functools.partial(leave_kernel, rows),
        in_specs=[SMEM] + [VMEM] * (MEMBERS + len(coming)),
        out_specs=VMEM,
        out_shape=jax.ShapeDtypeStruct((hp, 128, 128), BF16),
        scratch_shapes=[pltpu.VMEM((MEMBERS,) + last[0].shape, BF16)],
        compiler_params=SMALL,
        name="leave_quad",
    )(doc_lengths, *last, *coming)


def enter_kernel(rows, len_ref, *refs):
    in_ref, out_refs, last_ref, state_ref = refs[MEMBERS], refs[MEMBERS + 1 : -2], refs[-2], refs[-1]
    gather_last(refs[:MEMBERS], last_ref)
    hp = in_ref.shape[0]

    def note(i, e, state):
        state_ref[e, i] = state

    for i in range(hp):
        scan_quad(rows, len_ref, last_ref, in_ref[i].astype(F32), i, hp, functools.partial(note, i))
    me = lax.axis_index("seq") % MEMBERS
    for x, out_ref in enumerate(out_refs):
        out_ref[...] = state_ref[me ^ x].astype(BF16)


def enter_states(doc_lengths, last, coming, rows):
    return pl.pallas_call(
        functools.partial(enter_kernel, rows),
        in_specs=[SMEM] + [VMEM] * (MEMBERS + 1),
        out_specs=[VMEM] * MEMBERS,
        out_shape=[jax.ShapeDtypeStruct(coming.shape, BF16)] * MEMBERS,
        scratch_shapes=[
            pltpu.VMEM((MEMBERS,) + last[0].shape, BF16),
            pltpu.VMEM((MEMBERS,) + coming.shape, F32),
        ],
        compiler_params=SMALL,
        name="enter_states",
    )(doc_lengths, *last, coming)


def final_kernel(rows, len_ref, own_ref, *refs):
    side1_ref, side2_ref, in_ref, out_ref, last_ref, state_ref = refs[MEMBERS:]
    gather_last(refs[:MEMBERS], last_ref)
    hp = in_ref.shape[0]
    ends = read_ends(len_ref, len_ref.shape[0])
    base = lax.axis_index("seq") // MEMBERS * MEMBERS

    def note(i, e, state):
        state_ref[e, i] = state

    for i in range(hp):
        scan_quad(rows, len_ref, last_ref, in_ref[i].astype(F32), i, hp, functools.partial(note, i))
    out_ref[...] = jnp.zeros_like(out_ref)
    place, previous = jnp.int32(0), jnp.int32(-1)
    for d in range(len(ends)):
        device = (ends[d] - 1) // rows
        place = jnp.where(device == previous, place + 1, 0)
        previous = device
        at_end = ends[d] == (device + 1) * rows
        enters = (place == 0).astype(F32)
        mine = device // MEMBERS * MEMBERS == base
        e = device - base

        def put(i, local):
            state = local.astype(F32) + state_ref[e, i] * (decay_of(last_ref, e, i, hp) * enters)
            out_ref[own_ref[d], i] = state.astype(BF16)

        @pl.when(mine & at_end)
        def _():
            for i in range(hp):
                put(i, last_ref[e, i * 128 : (i + 1) * 128, :])

        @pl.when(mine & jnp.logical_not(at_end) & (place < SENT[0]))
        def _():
            for i in range(hp):
                put(i, side1_ref[e, pl.ds(pl.multiple_of((place * hp + i) * 128, 128), 128), :])

        @pl.when(mine & jnp.logical_not(at_end) & (place >= SENT[0]))
        def _():
            slot = jnp.minimum(place - SENT[0], SENT[1] - 1)
            for i in range(hp):
                put(i, side2_ref[e, pl.ds(pl.multiple_of((slot * hp + i) * 128, 128), 128), :])


def final_states(doc_lengths, owner_ids, last, side, coming, rows, spread):
    return pl.pallas_call(
        functools.partial(final_kernel, rows),
        in_specs=[SMEM, SMEM] + [VMEM] * (MEMBERS + 3),
        out_specs=VMEM,
        out_shape=jax.ShapeDtypeStruct((spread,) + coming.shape, BF16),
        scratch_shapes=[
            pltpu.VMEM((MEMBERS,) + last[0].shape, BF16),
            pltpu.VMEM((MEMBERS,) + coming.shape, F32),
        ],
        compiler_params=SMALL,
        name="final_states",
    )(doc_lengths, owner_ids, *last, *side, coming)


def finish_kernel(
    len_ref, q_ref, k_ref, v_ref, e0, e1, e2, e3, local_ref, gate_ref, gain_ref, crow_ref, out_ref, bias_ref, ccol_ref
):
    rows = q_ref.shape[0]
    step = pl.program_id(0)
    me = lax.axis_index("seq")
    first = me * rows
    ends = read_ends(len_ref, len_ref.shape[0])
    hp = e0.shape[0]
    pairs = sum(EARLY) // 2

    def entering(h):
        far = (h // hp) ^ (me % MEMBERS)
        state = e0[h % hp]
        for x, ref in ((1, e1), (2, e2), (3, e3)):
            state = jnp.where(far == x, ref[h % hp], state)
        return state

    def emit(lanes, t0, size, att):
        mean = jnp.mean(att * att, axis=1, keepdims=True)
        gate = 0.5 + 0.5 * jnp.tanh(0.5 * gate_ref[t0 : t0 + size, lanes].astype(F32))
        gain = gain_ref[:, lanes].astype(F32)
        out_ref[t0 : t0 + size, lanes] = (att * lax.rsqrt(mean + 1e-06) * (gain * gate)).astype(BF16)

    @pl.when(step == 0)
    def _():
        fill_bias(first, ends, bias_ref)
        fill_columns(crow_ref, ccol_ref)

    @pl.when(step < pairs)
    def _():
        reach = run_end(ends, first - 1) - first
        cols = [head_column(ccol_ref, step * 2 + i) for i in range(2)]
        states = [entering(step * 2 + i) for i in range(2)]
        lanes = [slice(i * 128, (i + 1) * 128) for i in range(2)]
        for t0 in range(0, rows, 256):
            carry = [dot(q_ref[t0 : t0 + 256, lanes[i]], states[i]) for i in range(2)]
            at = t0 + iota((256, 1), 0)
            for i in range(2):
                lead = jnp.exp2(jnp.where(at < reach, cols[i][t0 : t0 + 256], NEG))
                emit(lanes[i], t0, 256, local_ref[t0 : t0 + 256, lanes[i]] + lead * carry[i])

    @pl.when(step >= pairs)
    def _():
        states = [entering(step * 2 + i).astype(F32) for i in range(2)]
        attend(first, ends, q_ref, k_ref, v_ref, step * 2, crow_ref, ccol_ref, bias_ref, states, emit)


def finish(doc_lengths, queries, keys, values, entering, local, gate, gain, crow):
    heads, rows = crow.shape
    pairs = sum(EARLY) // 2
    wide = pl.BlockSpec((rows, 256), lambda j: (0, j))
    late = pl.BlockSpec((rows, 256), lambda j: (0, jnp.maximum(j, pairs)))
    return pl.pallas_call(
        finish_kernel,
        grid=(heads // 2,),
        in_specs=[SMEM, wide, late, late]
        + [whole(e.shape) for e in entering]
        + [
            pl.BlockSpec((rows, 256), lambda j: (0, jnp.minimum(j, pairs - 1))),
            wide,
            pl.BlockSpec((1, 256), lambda j: (0, j)),
            whole((heads, rows)),
        ],
        out_specs=wide,
        out_shape=jax.ShapeDtypeStruct((rows, heads * 128), BF16),
        scratch_shapes=[pltpu.VMEM((rows, CHUNK), F32), pltpu.VMEM((rows, 128), F32)],
        compiler_params=LIMIT,
        cost_estimate=pl.CostEstimate(
            flops=heads * rows * CHUNK * 128 * 8, bytes_accessed=rows * heads * 128 * 10, transcendentals=heads * rows * CHUNK
        ),
        name="finish",
    )(doc_lengths, queries, keys, values, *entering, local, gate, gain, crow)


def swap(x, groups=None):
    return lax.all_to_all(x, "seq", split_axis=0, concat_axis=0, axis_index_groups=groups, tiled=True)


def by_distance(parcels, spread):
    return [parcels[0]] + [
        lax.ppermute(parcels[x], "seq", [(s, s ^ x) for s in range(spread)]) for x in range(1, MEMBERS)
    ]


def on_device(spread, queries, keys, values, log_decay, gate, gain, doc_lengths, owner_ids):
    rows, heads = log_decay.shape
    quads = spread // MEMBERS
    hp = heads // MEMBERS
    near = [[q * MEMBERS + m for m in range(MEMBERS)] for q in range(quads)]
    onward = [(s, s + MEMBERS) for s in range(spread - MEMBERS)]
    decay_rows = log_decay.T
    barrier = lax.optimization_barrier

    side1, side2, crow, flags, *last = piece_states(doc_lengths, owner_ids, decay_rows, keys, values)
    early = functools.partial(early_attention, doc_lengths, queries, keys, values)
    last = by_distance(last, spread)
    side1, last[1] = barrier((side1, last[1]))
    side1 = swap(side1, near)
    local = early(crow, [], 0)
    last, local = barrier((last, local))

    coming = []
    for _ in range(quads - 1):
        leaving = leave_quad(doc_lengths, last, coming, rows, hp)
        coming = [lax.ppermute(leaving, "seq", onward)]
    crow_1, leaving = barrier((crow, leaving))
    local = early(crow_1, [local], 1)
    side1, side2, local, flags, gain = barrier((side1, side2, local, flags, gain))
    side2 = swap(side2, near)
    gain = gain.reshape(1, -1)

    def send_rest():
        rest, _ = piece_states(doc_lengths, owner_ids, decay_rows, keys, values, spread)
        return lax.dynamic_index_in_dim(swap(rest), flags[3], 0, True)

    rest = lax.cond(flags[2] > 0, send_rest, lambda: jnp.zeros((1, heads, 128, 128), BF16))
    from_quad = [flags[0] == q for q in range(1, quads)]
    coming, rest, gain, late, from_quad, local = barrier((coming[0], rest, gain, flags[1] > 0, from_quad, local))

    entering = by_distance(enter_states(doc_lengths, last, coming, rows), spread)
    finals = final_states(doc_lengths, owner_ids, last, [side1, side2], coming, rows, spread)
    entering[1], finals = barrier((entering[1], finals))
    arrived = swap(finals).reshape(quads, 1, heads, 128, 128)
    entering, finals = barrier((entering, finals))
    mixed = finish(doc_lengths, queries, keys, values, entering, local, gate, gain, crow)
    owned = arrived[0]
    for q in range(1, quads):
        owned = jnp.where(from_quad[q - 1], arrived[q], owned)
    return mixed, jnp.where(late, rest, owned)


def solution(mesh):
    placed = (
        P(("groups", "seq"), "tp"),
        P(("groups", "seq"), "tp"),
        P(("groups", "seq"), "tp"),
        P(("groups", "seq"), "tp"),
        P(("groups", "seq"), "tp"),
        P("tp"),
        P("groups"),
        P("groups"),
    )
    return jax.shard_map(
        functools.partial(on_device, mesh.shape["seq"]),
        mesh=mesh,
        in_specs=placed,
        out_specs=(P(("groups", "seq"), "tp"), P(("groups", "seq"), "tp", None, None)),
        check_vma=False,
    )
```

profile of v0, /device:TPU:0, one launch (start us, length us, event | category | flops | bytes accessed | tf_op | source)
XLA Modules:
  0.0 109.7 jit_solution(10117914488789144696)
XLA Ops:
  0.6 0.0 copy-start.6
  0.6 7.5 %piece_states.3 = (bf16[4,1024,128]{2,1,0:T(8,128)(2,1)}, bf16[4,512,128]{2,1,0:T(8,128)(2,1)}, f32[16,1024]{1,0:T(8,128)}, s32[4]{0:T(128)S(1)}, bf16[528,128]{...) custom-call(s32[8]{0:T(128)} %len_ref.13, s32[8]{0:T(128)} %own_ref.3, ...), custom_call_target="tpu_custom_call" | custom-call | flops 1073741824 | bytes 8388608 | tf_op jit(solution)/shard_map/piece_states/pallas_call | solution.py:241
  8.1 3.0 %collective-permute-start = (bf16[528,128]{1,0:T(8,128)(2,1)}, bf16[528,128]{1,0:T(8,128)(2,1)S(1)}, u32[]{:S(2)}, u32[]{:S(2)}) collective-permute-start(bf16[528,128]{1,0:T(8,128)(2,1)} %get-tuple-element.63), channel_id=1, source_target_pairs={{0,2},{2,0},{4,6},{6,4},{8,10},{10,8},{12,14},{14,12},{1,3},{3,1},... | collective-permute-start | bytes 405512 | tf_op jit(solution)/shard_map/ppermute | solution.py:601
  11.1 3.8 %collective-permute-done.refs_1_ = bf16[528,128]{1,0:T(8,128)(2,1)S(1)} collective-permute-done((bf16[528,128]{1,0:T(8,128)(2,1)}, bf16[528,128]{1,0:T(8,128)(2,1)S(1)}, u32[]{:S(2)}, u32[]{:S(2)}) %collective-permute-start) | collective-permute-done | bytes 135200 | tf_op jit(solution)/shard_map/ppermute | solution.py:601
  14.9 4.0 %all-to-all-start.1 = ((bf16[4,1024,128]{2,1,0:T(8,128)(2,1)}), bf16[4,1024,128]{2,1,0:T(8,128)(2,1)S(1)}, u32[]{:S(2)}, u32[]{:S(2)}) async-start(bf16[4,1024,128]{2,1,0:T(8,128)(2,1)} %get-tuple-element.72), calls=%async_computation.1 | async-start | bytes 2097152 | tf_op jit(solution)/shard_map/all_to_all | solution.py:596
  18.9 2.0 %collective-permute-start.1 = (bf16[528,128]{1,0:T(8,128)(2,1)}, bf16[528,128]{1,0:T(8,128)(2,1)S(1)}, u32[]{:S(2)}, u32[]{:S(2)}) collective-permute-start(bf16[528,128]{1,0:T(8,128)(2,1)} %get-tuple-element.65), channel_id=1, source_target_pairs={{0,4},{2,6},{4,0},{6,2},{8,12},{10,14},{12,8},{14,10},{1,5},{3,7},... | collective-permute-start | bytes 405512 | tf_op jit(solution)/shard_map/ppermute | solution.py:601
  21.0 1.5 %collective-permute-start.2 = (bf16[528,128]{1,0:T(8,128)(2,1)}, bf16[528,128]{1,0:T(8,128)(2,1)S(1)}, u32[]{:S(2)}, u32[]{:S(2)}) collective-permute-start(bf16[528,128]{1,0:T(8,128)(2,1)} %get-tuple-element.66), channel_id=1, source_target_pairs={{0,6},{2,4},{4,2},{6,0},{8,14},{10,12},{12,10},{14,8},{1,7},{3,5},... | collective-permute-start | bytes 405512 | tf_op jit(solution)/shard_map/ppermute | solution.py:601
  22.4 0.0 copy-done.6
  22.4 0.0 copy-start
  22.4 5.2 %early_attention.2.refs_0_ = f32[1024,1024]{1,0:T(8,128)} custom-call(s32[8]{0:T(128)S(1)} %copy-done.6, bf16[1024,2048]{1,0:T(8,128)(2,1)} %q_ref.5, bf16[1024,2048]{1,0:T(8,128)(2,1)} %k_ref.7, bf16[1024,2048]{1,0:T(8,128)(2,1)} %v_ref.7, f32[16,1024]{1,0:T(8,128)} %get-tuple-element.74.crow_ref), custom_call_target="tpu_custom_call" | custom-call | flops 1073741824 | bytes 5242880 | tf_op jit(solution)/shard_map/early_attention/pallas_call | solution.py:364
  27.6 8.5 %collective-permute-done.1.refs_2_ = bf16[528,128]{1,0:T(8,128)(2,1)S(1)} collective-permute-done((bf16[528,128]{1,0:T(8,128)(2,1)}, bf16[528,128]{1,0:T(8,128)(2,1)S(1)}, u32[]{:S(2)}, u32[]{:S(2)}) %collective-permute-start.1) | collective-permute-done | bytes 135200 | tf_op jit(solution)/shard_map/ppermute | solution.py:601
  36.1 2.3 %collective-permute-done.2.refs_3_ = bf16[528,128]{1,0:T(8,128)(2,1)S(1)} collective-permute-done((bf16[528,128]{1,0:T(8,128)(2,1)}, bf16[528,128]{1,0:T(8,128)(2,1)S(1)}, u32[]{:S(2)}, u32[]{:S(2)}) %collective-permute-start.2) | collective-permute-done | bytes 135200 | tf_op jit(solution)/shard_map/ppermute | solution.py:601
  38.5 0.0 copy-done
  38.5 0.7 leave_quad.1
  39.2 0.0 copy-start.2
  39.2 0.0 copy-start.7
  39.2 5.2 %early_attention.3.local_ref = f32[1024,1024]{1,0:T(8,128)} custom-call(s32[8]{0:T(128)S(1)} %copy-done.6, bf16[1024,2048]{1,0:T(8,128)(2,1)} %q_ref.5, bf16[1024,2048]{1,0:T(8,128)(2,1)} %k_ref.7, bf16[1024,2048]{1,0:T(8,128)(2,1)} %v_ref.7, f32[16,1024]{1,0:T(8,128)} %get-tuple-element.74.crow_ref, ...), custom_call_target="tpu_custom_call", output_to_operand_aliasing={{}: (5, {})} | custom-call | flops 1073741824 | bytes 5242880 | tf_op jit(solution)/shard_map/early_attention/pallas_call | solution.py:364
  44.4 0.0 all-to-all-done.1.refs_4_
  44.4 0.6 fusion
  45.7 0.0 copy-done.2
  45.7 0.0 copy-done.7
  45.7 0.0 copy-start.8
  45.7 0.1 conditional.1
  45.7 0.1 broadcast.12
  45.8 3.5 %all-to-all-start.2 = ((bf16[4,512,128]{2,1,0:T(8,128)(2,1)}), bf16[4,512,128]{2,1,0:T(8,128)(2,1)S(1)}, u32[]{:S(2)}, u32[]{:S(2)}) async-start(bf16[4,512,128]{2,1,0:T(8,128)(2,1)} %get-tuple-element.84), calls=%async_computation.2 | async-start | bytes 1048576 | tf_op jit(solution)/shard_map/all_to_all | solution.py:596
  49.3 4.5 %collective-permute-start.3 = (bf16[4,128,128]{2,1,0:T(8,128)(2,1)S(1)}, bf16[4,128,128]{2,1,0:T(8,128)(2,1)S(1)}, u32[]{:S(2)}, u32[]{:S(2)}) collective-permute-start(bf16[4,128,128]{2,1,0:T(8,128)(2,1)S(1)} %leave_quad.1), channel_id=1, source_target_pairs={{0,8},{2,10},{4,12},{6,14},{1,9},{3,11},{5,13},{7,15},{16,24},{18,... | collective-permute-start | bytes 393224 | tf_op jit(solution)/shard_map/ppermute | solution.py:625
  53.8 0.0 copy-done.8
  53.8 0.6 reshape.42.gain_ref
  55.6 0.7 collective-permute-done.3.refs_4_.refs_6_
  56.3 0.8 enter_states.1
  57.0 0.0 copy-start.1
  57.1 0.6 copy-done.1
  57.7 2.0 %collective-permute-start.4 = (bf16[4,128,128]{2,1,0:T(8,128)(2,1)S(1)}, bf16[4,128,128]{2,1,0:T(8,128)(2,1)S(1)}, u32[]{:S(2)}, u32[]{:S(2)}) collective-permute-start(bf16[4,128,128]{2,1,0:T(8,128)(2,1)S(1)} %get-tuple-element.82), channel_id=1, source_target_pairs={{0,2},{2,0},{4,6},{6,4},{8,10},{10,8},{12,14},{14,12},{1,3},{3,1},... | collective-permute-start | bytes 393224 | tf_op jit(solution)/shard_map/ppermute | solution.py:601
  59.7 0.0 all-to-all-done.2.refs_5_
  59.7 2.1 %final_states.1 = bf16[8,4,128,128]{3,2,1,0:T(8,128)(2,1)} custom-call(s32[8]{0:T(128)S(1)} %copy-done.6, s32[8]{0:T(128)S(1)} %copy-done.7, bf16[528,128]{1,0:T(8,128)(2,1)S(1)} %copy-done, bf16[528,128]{1,0:T(8,128)(2,1)S(1)} %collective-permute-done.refs_1_, bf16[528,128]{1,0:T(8,128)(2,1)S(1)} %collective-permute-done.1.refs_2_, ...), custom_call_target="tpu_custom_call" | custom-call | tf_op jit(solution)/shard_map/final_states/pallas_call | solution.py:506
  61.8 0.9 collective-permute-done.4.e1
  62.7 8.3 %all-to-all-start.3 = ((bf16[8,4,128,128]{3,2,1,0:T(8,128)(2,1)}), bf16[8,4,128,128]{3,2,1,0:T(8,128)(2,1)S(1)}, u32[]{:S(2)}, u32[]{:S(2)}) async-start(bf16[8,4,128,128]{3,2,1,0:T(8,128)(2,1)} %final_states.1), calls=%async_computation.3 | async-start | bytes 2097152 | tf_op jit(solution)/shard_map/all_to_all | solution.py:596
  71.0 2.0 %collective-permute-start.5 = (bf16[4,128,128]{2,1,0:T(8,128)(2,1)S(1)}, bf16[4,128,128]{2,1,0:T(8,128)(2,1)S(1)}, u32[]{:S(2)}, u32[]{:S(2)}) collective-permute-start(bf16[4,128,128]{2,1,0:T(8,128)(2,1)S(1)} %get-tuple-element.86), channel_id=1, source_target_pairs={{0,4},{2,6},{4,0},{6,2},{8,12},{10,14},{12,8},{14,10},{1,5},{3,7},... | collective-permute-start | bytes 393224 | tf_op jit(solution)/shard_map/ppermute | solution.py:601
  73.0 1.5 %collective-permute-start.6 = (bf16[4,128,128]{2,1,0:T(8,128)(2,1)S(1)}, bf16[4,128,128]{2,1,0:T(8,128)(2,1)S(1)}, u32[]{:S(2)}, u32[]{:S(2)}) collective-permute-start(bf16[4,128,128]{2,1,0:T(8,128)(2,1)S(1)} %get-tuple-element.87), channel_id=1, source_target_pairs={{0,6},{2,4},{4,2},{6,0},{8,14},{10,12},{12,10},{14,8},{1,7},{3,5},... | collective-permute-start | bytes 393224 | tf_op jit(solution)/shard_map/ppermute | solution.py:601
  74.5 13.6 %collective-permute-done.5.e2 = bf16[4,128,128]{2,1,0:T(8,128)(2,1)S(1)} collective-permute-done((bf16[4,128,128]{2,1,0:T(8,128)(2,1)S(1)}, bf16[4,128,128]{2,1,0:T(8,128)(2,1)S(1)}, u32[]{:S(2)}, u32[]{:S(2)}) %collective-permute-start.5) | collective-permute-done | bytes 131104 | tf_op jit(solution)/shard_map/ppermute | solution.py:601
  88.1 2.4 %collective-permute-done.6.e3 = bf16[4,128,128]{2,1,0:T(8,128)(2,1)S(1)} collective-permute-done((bf16[4,128,128]{2,1,0:T(8,128)(2,1)S(1)}, bf16[4,128,128]{2,1,0:T(8,128)(2,1)S(1)}, u32[]{:S(2)}, u32[]{:S(2)}) %collective-permute-start.6) | collective-permute-done | bytes 131104 | tf_op jit(solution)/shard_map/ppermute | solution.py:601
  90.5 0.0 copy-done.3
  90.5 0.0 copy-done.4
  90.5 0.6 copy-done.5
  91.2 17.6 %finish.1 = bf16[1024,2048]{1,0:T(8,128)(2,1)} custom-call(s32[8]{0:T(128)S(1)} %copy-done.6, bf16[1024,2048]{1,0:T(8,128)(2,1)} %q_ref.5, bf16[1024,2048]{1,0:T(8,128)(2,1)} %k_ref.7, bf16[1024,2048]{1,0:T(8,128)(2,1)} %v_ref.7, bf16[4,128,128]{2,1,0:T(8,128)(2,1)} %copy-done.1, bf16[4,128,128]{2,1,0:T(8,128)(2,1)} %copy-done.3, ...), custom_call_target="tpu_custom_call" | custom-call | flops 4294967296 | bytes 20971520 | tf_op jit(solution)/shard_map/finish/pallas_call | solution.py:573
  108.8 0.0 all-to-all-done.3
  108.8 0.1 slice_select_fusion
  108.9 0.9 bitcast_select_fusion
  (3 shorter events, 0.0 us)
Async XLA Ops:
  0.6 21.8 %copy-start.6 = (s32[8]{0:T(128)S(1)}, s32[8]{0:T(128)}, u32[]{:S(2)}) copy-start(s32[8]{0:T(128)} %len_ref.13) | copy-start | bytes 100
  8.1 6.8 %collective-permute-start = (bf16[528,128]{1,0:T(8,128)(2,1)}, bf16[528,128]{1,0:T(8,128)(2,1)S(1)}, u32[]{:S(2)}, u32[]{:S(2)}) collective-permute-start(bf16[528,128]{1,0:T(8,128)(2,1)} %get-tuple-element.63), channel_id=1, source_target_pairs={{0,2},{2,0},{4,6},{6,4},{8,10},{10,8},{12,14},{14,12},{1,3},{3,1},... | collective-permute-start | bytes 405512 | tf_op jit(solution)/shard_map/ppermute | solution.py:601
  14.9 29.5 %all-to-all-start.1 = ((bf16[4,1024,128]{2,1,0:T(8,128)(2,1)}), bf16[4,1024,128]{2,1,0:T(8,128)(2,1)S(1)}, u32[]{:S(2)}, u32[]{:S(2)}) async-start(bf16[4,1024,128]{2,1,0:T(8,128)(2,1)} %get-tuple-element.72), calls=%async_computation.1 | async-start | bytes 2097152 | tf_op jit(solution)/shard_map/all_to_all | solution.py:596
  18.9 17.2 %collective-permute-start.1 = (bf16[528,128]{1,0:T(8,128)(2,1)}, bf16[528,128]{1,0:T(8,128)(2,1)S(1)}, u32[]{:S(2)}, u32[]{:S(2)}) collective-permute-start(bf16[528,128]{1,0:T(8,128)(2,1)} %get-tuple-element.65), channel_id=1, source_target_pairs={{0,4},{2,6},{4,0},{6,2},{8,12},{10,14},{12,8},{14,10},{1,5},{3,7},... | collective-permute-start | bytes 405512 | tf_op jit(solution)/shard_map/ppermute | solution.py:601
  21.0 17.5 %collective-permute-start.2 = (bf16[528,128]{1,0:T(8,128)(2,1)}, bf16[528,128]{1,0:T(8,128)(2,1)S(1)}, u32[]{:S(2)}, u32[]{:S(2)}) collective-permute-start(bf16[528,128]{1,0:T(8,128)(2,1)} %get-tuple-element.66), channel_id=1, source_target_pairs={{0,6},{2,4},{4,2},{6,0},{8,14},{10,12},{12,10},{14,8},{1,7},{3,5},... | collective-permute-start | bytes 405512 | tf_op jit(solution)/shard_map/ppermute | solution.py:601
  22.4 16.0 %copy-start = (bf16[528,128]{1,0:T(8,128)(2,1)S(1)}, bf16[528,128]{1,0:T(8,128)(2,1)}, u32[]{:S(2)}) copy-start(bf16[528,128]{1,0:T(8,128)(2,1)} %get-tuple-element.68.refs_0_) | copy-start | bytes 405508
  39.2 6.5 %copy-start.2 = (f32[1024,16]{0,1:T(8,128)S(1)}, f32[1024,16]{0,1:T(8,128)}, u32[]{:S(2)}) copy-start(f32[1024,16]{0,1:T(8,128)} %param.13) | copy-start | bytes 196612
  39.2 6.5 %copy-start.7 = (s32[8]{0:T(128)S(1)}, s32[8]{0:T(128)}, u32[]{:S(2)}) copy-start(s32[8]{0:T(128)} %own_ref.3) | copy-start | bytes 100
  45.7 8.1 %copy-start.8 = (bf16[2048]{0:T(1024)(128)(2,1)S(1)}, bf16[2048]{0:T(1024)(128)(2,1)}, u32[]{:S(2)}) copy-start(bf16[2048]{0:T(1024)(128)(2,1)} %param.15) | copy-start | bytes 12292
  45.8 13.8 %all-to-all-start.2 = ((bf16[4,512,128]{2,1,0:T(8,128)(2,1)}), bf16[4,512,128]{2,1,0:T(8,128)(2,1)S(1)}, u32[]{:S(2)}, u32[]{:S(2)}) async-start(bf16[4,512,128]{2,1,0:T(8,128)(2,1)} %get-tuple-element.84), calls=%async_computation.2 | async-start | bytes 1048576 | tf_op jit(solution)/shard_map/all_to_all | solution.py:596
  49.3 7.0 %collective-permute-start.3 = (bf16[4,128,128]{2,1,0:T(8,128)(2,1)S(1)}, bf16[4,128,128]{2,1,0:T(8,128)(2,1)S(1)}, u32[]{:S(2)}, u32[]{:S(2)}) collective-permute-start(bf16[4,128,128]{2,1,0:T(8,128)(2,1)S(1)} %leave_quad.1), channel_id=1, source_target_pairs={{0,8},{2,10},{4,12},{6,14},{1,9},{3,11},{5,13},{7,15},{16,24},{18,... | collective-permute-start | bytes 393224 | tf_op jit(solution)/shard_map/ppermute | solution.py:625
  57.0 0.7 copy-start.1
  57.7 5.0 %collective-permute-start.4 = (bf16[4,128,128]{2,1,0:T(8,128)(2,1)S(1)}, bf16[4,128,128]{2,1,0:T(8,128)(2,1)S(1)}, u32[]{:S(2)}, u32[]{:S(2)}) collective-permute-start(bf16[4,128,128]{2,1,0:T(8,128)(2,1)S(1)} %get-tuple-element.82), channel_id=1, source_target_pairs={{0,2},{2,0},{4,6},{6,4},{8,10},{10,8},{12,14},{14,12},{1,3},{3,1},... | collective-permute-start | bytes 393224 | tf_op jit(solution)/shard_map/ppermute | solution.py:601
  62.7 27.9 %copy-start.3 = (bf16[4,128,128]{2,1,0:T(8,128)(2,1)}, bf16[4,128,128]{2,1,0:T(8,128)(2,1)S(1)}, u32[]{:S(2)}) copy-start(bf16[4,128,128]{2,1,0:T(8,128)(2,1)S(1)} %collective-permute-done.4.e1) | copy-start | bytes 393220
  62.7 46.1 %all-to-all-start.3 = ((bf16[8,4,128,128]{3,2,1,0:T(8,128)(2,1)}), bf16[8,4,128,128]{3,2,1,0:T(8,128)(2,1)S(1)}, u32[]{:S(2)}, u32[]{:S(2)}) async-start(bf16[8,4,128,128]{3,2,1,0:T(8,128)(2,1)} %final_states.1), calls=%async_computation.3 | async-start | bytes 2097152 | tf_op jit(solution)/shard_map/all_to_all | solution.py:596
  71.0 17.1 %collective-permute-start.5 = (bf16[4,128,128]{2,1,0:T(8,128)(2,1)S(1)}, bf16[4,128,128]{2,1,0:T(8,128)(2,1)S(1)}, u32[]{:S(2)}, u32[]{:S(2)}) collective-permute-start(bf16[4,128,128]{2,1,0:T(8,128)(2,1)S(1)} %get-tuple-element.86), channel_id=1, source_target_pairs={{0,4},{2,6},{4,0},{6,2},{8,12},{10,14},{12,8},{14,10},{1,5},{3,7},... | collective-permute-start | bytes 393224 | tf_op jit(solution)/shard_map/ppermute | solution.py:601
  73.0 17.5 %collective-permute-start.6 = (bf16[4,128,128]{2,1,0:T(8,128)(2,1)S(1)}, bf16[4,128,128]{2,1,0:T(8,128)(2,1)S(1)}, u32[]{:S(2)}, u32[]{:S(2)}) collective-permute-start(bf16[4,128,128]{2,1,0:T(8,128)(2,1)S(1)} %get-tuple-element.87), channel_id=1, source_target_pairs={{0,6},{2,4},{4,2},{6,0},{8,14},{10,12},{12,10},{14,8},{1,7},{3,5},... | collective-permute-start | bytes 393224 | tf_op jit(solution)/shard_map/ppermute | solution.py:601
  88.1 2.4 %copy-start.4 = (bf16[4,128,128]{2,1,0:T(8,128)(2,1)}, bf16[4,128,128]{2,1,0:T(8,128)(2,1)S(1)}, u32[]{:S(2)}) copy-start(bf16[4,128,128]{2,1,0:T(8,128)(2,1)S(1)} %collective-permute-done.5.e2) | copy-start | bytes 393220
  90.5 0.6 copy-start.5
where the time goes:
time: 110 us
  Pallas kernels  39.1 us (36%)
  starting transfers between devices  32.2 us (29%)
  waiting for transfers between devices  32.2 us (29%)
  between operations  2.63 us (2%)
  local copies, waits for them, and re-layouts  2.62 us (2%)
    ppermute x6, waiting for transfers between devices, by_distance(): lax.ppermute(parcels[x], 'seq', [(s, s ^ x) for s in range(spread)])  31.5 us
    pallas_call x1, Pallas kernels, finish(): pl.pallas_call(finish_kernel, grid=(heads // 2,), in_specs=[SMEM, wide, l...  17.6 us
    all_to_all x3, starting transfers between devices, swap(): lax.all_to_all(x, 'seq', split_axis=0, concat_axis=0, axis_index_groups=g...  15.8 us
    ppermute x6, starting transfers between devices, by_distance(): lax.ppermute(parcels[x], 'seq', [(s, s ^ x) for s in range(spread)])  11.9 us
    pallas_call x2, Pallas kernels, early_attention(): pl.pallas_call(functools.partial(early_kernel, skip), grid=(count // 2,),...  10.4 us
    pallas_call x1, Pallas kernels, piece_states(): pl.pallas_call(functools.partial(pieces_kernel, by_owner), grid=(heads //...  7.49 us
    ppermute x1, starting transfers between devices, on_device(): coming = [lax.ppermute(leaving, 'seq', onward)]  4.45 us
  transfers between devices with their start and end apart: 10, of which 7 were waited for; matrix products, arithmetic and copies ran while one was open for 1% of the time, Pallas kernels for 29%

commit v1 on v0

--- a/solution.py
+++ b/solution.py
@@ -10,12 +10,11 @@
 
 BLK = 512
 SIDE = 3
-SENT = (2, 1)
 EXTRA = 16
 CHUNK = 256
 MEMBERS = 4
 TILE = 256
-EARLY = (4, 4)
+EARLY = (8,)
 NEG = -1e30
 LOG2E = math.log2(math.e)
 SCALE = 128**-0.5
@@ -98,9 +97,9 @@
         side_ref, crow_ref, w_ref, keep_ref = refs
         slots = keep_ref.shape[0]
     else:
-        side_refs, crow_ref, flag_ref = refs[:2], refs[2], refs[3]
-        last_refs = refs[4 : 4 + MEMBERS]
-        w_ref, first_ref, high_ref, weighted_ref, prefix_ref = refs[4 + MEMBERS :]
+        side_ref, crow_ref, flag_ref = refs[:3]
+        last_refs = refs[3 : 3 + MEMBERS]
+        w_ref, first_ref, high_ref, weighted_ref, prefix_ref = refs[3 + MEMBERS :]
         slots = SIDE
     heads, rows = crow_ref.shape
     step = pl.program_id(0)
@@ -189,14 +188,13 @@
         tile = jnp.maximum(high, 0) // TILE
         start = pl.multiple_of(tile * TILE, TILE)
         keep = jnp.where(start + iota((16, TILE), 1) <= high, 1.0, 0.0).astype(BF16)
-        part, slot = (0, s) if s < SENT[0] else (1, s - SENT[0])
         for i in pairs:
             kept = weighted_ref[lanes[i], pl.ds(start, TILE)].reshape(16, 16, TILE) * keep[None]
             states = dot(kept.reshape(256, TILE), v_ref[pl.ds(start, TILE), lanes[i]])
             for j in range(2):
                 until = own(states, j) + prefix_ref[tile, i + j]
-                at = (slot * hp + i + j) * 128
-                side_refs[part][0, at : at + 128, :] = (until - ended[i][j]).astype(BF16)
+                at = (s * hp + i + j) * 128
+                side_ref[0, at : at + 128, :] = (until - ended[i][j]).astype(BF16)
                 ended[i][j] = until
     rate = first_ref[pl.ds(step * hp, hp), :]
     high = rate.astype(BF16).astype(F32)
@@ -225,13 +223,13 @@
     else:
         last = (hp * 128 + EXTRA, 128)
         shapes = [
-            *[jax.ShapeDtypeStruct((MEMBERS, n * hp * 128, 128), BF16) for n in SENT],
+            jax.ShapeDtypeStruct((MEMBERS, SIDE * hp * 128, 128), BF16),
             jax.ShapeDtypeStruct((heads, rows), F32),
             jax.ShapeDtypeStruct((4,), jnp.int32),
             *[jax.ShapeDtypeStruct(last, BF16)] * MEMBERS,
         ]
-        specs = [pl.BlockSpec((1, n * hp * 128, 128), lambda j: (j, 0, 0)) for n in SENT]
-        specs += [whole((heads, rows)), SMEM] + [whole(last)] * MEMBERS
+        specs = [pl.BlockSpec((1, SIDE * hp * 128, 128), lambda j: (j, 0, 0)), whole((heads, rows)), SMEM]
+        specs += [whole(last)] * MEMBERS
         scratch += [
             pltpu.VMEM((heads, 128), F32),
             pltpu.SMEM((SIDE,), jnp.int32),
@@ -377,6 +375,11 @@
     )(doc_lengths, queries, keys, values, crow, *before)
 
 
+def from_before(in_ref, i):
+    quad = lax.axis_index("seq") // MEMBERS
+    return in_ref[jnp.maximum(quad - 1, 0), i].astype(F32) * (quad > 0).astype(F32)
+
+
 def gather_last(refs, last_ref):
     me = lax.axis_index("seq") % MEMBERS
     for x, ref in enumerate(refs):
@@ -411,7 +414,7 @@
     for i in range(hp):
         state = jnp.zeros((128, 128), F32)
         if len(refs) > MEMBERS + 2:
-            state = refs[MEMBERS][i].astype(F32)
+            state = from_before(refs[MEMBERS], i)
         state = scan_quad(rows, len_ref, last_ref, state, i, hp, lambda e, x: None)
         out_ref[i] = state.astype(BF16)
 
@@ -431,13 +434,13 @@
 def enter_kernel(rows, len_ref, *refs):
     in_ref, out_refs, last_ref, state_ref = refs[MEMBERS], refs[MEMBERS + 1 : -2], refs[-2], refs[-1]
     gather_last(refs[:MEMBERS], last_ref)
-    hp = in_ref.shape[0]
+    hp = in_ref.shape[1]
 
     def note(i, e, state):
         state_ref[e, i] = state
 
     for i in range(hp):
-        scan_quad(rows, len_ref, last_ref, in_ref[i].astype(F32), i, hp, functools.partial(note, i))
+        scan_quad(rows, len_ref, last_ref, from_before(in_ref, i), i, hp, functools.partial(note, i))
     me = lax.axis_index("seq") % MEMBERS
     for x, out_ref in enumerate(out_refs):
         out_ref[...] = state_ref[me ^ x].astype(BF16)
@@ -448,10 +451,10 @@
         functools.partial(enter_kernel, rows),
         in_specs=[SMEM] + [VMEM] * (MEMBERS + 1),
         out_specs=[VMEM] * MEMBERS,
-        out_shape=[jax.ShapeDtypeStruct(coming.shape, BF16)] * MEMBERS,
+        out_shape=[jax.ShapeDtypeStruct(coming.shape[1:], BF16)] * MEMBERS,
         scratch_shapes=[
             pltpu.VMEM((MEMBERS,) + last[0].shape, BF16),
-            pltpu.VMEM((MEMBERS,) + coming.shape, F32),
+            pltpu.VMEM((MEMBERS,) + coming.shape[1:], F32),
         ],
         compiler_params=SMALL,
         name="enter_states",
@@ -459,9 +462,9 @@
 
 
 def final_kernel(rows, len_ref, own_ref, *refs):
-    side1_ref, side2_ref, in_ref, out_ref, last_ref, state_ref = refs[MEMBERS:]
+    side_ref, in_ref, out_ref, last_ref, state_ref = refs[MEMBERS:]
     gather_last(refs[:MEMBERS], last_ref)
-    hp = in_ref.shape[0]
+    hp = in_ref.shape[1]
     ends = read_ends(len_ref, len_ref.shape[0])
     base = lax.axis_index("seq") // MEMBERS * MEMBERS
 
@@ -469,7 +472,7 @@
         state_ref[e, i] = state
 
     for i in range(hp):
-        scan_quad(rows, len_ref, last_ref, in_ref[i].astype(F32), i, hp, functools.partial(note, i))
+        scan_quad(rows, len_ref, last_ref, from_before(in_ref, i), i, hp, functools.partial(note, i))
     out_ref[...] = jnp.zeros_like(out_ref)
     place, previous = jnp.int32(0), jnp.int32(-1)
     for d in range(len(ends)):
@@ -490,31 +493,26 @@
             for i in range(hp):
                 put(i, last_ref[e, i * 128 : (i + 1) * 128, :])
 
-        @pl.when(mine & jnp.logical_not(at_end) & (place < SENT[0]))
+        @pl.when(mine & jnp.logical_not(at_end))
         def _():
             for i in range(hp):
-                put(i, side1_ref[e, pl.ds(pl.multiple_of((place * hp + i) * 128, 128), 128), :])
-
-        @pl.when(mine & jnp.logical_not(at_end) & (place >= SENT[0]))
-        def _():
-            slot = jnp.minimum(place - SENT[0], SENT[1] - 1)
-            for i in range(hp):
-                put(i, side2_ref[e, pl.ds(pl.multiple_of((slot * hp + i) * 128, 128), 128), :])
+                row = pl.multiple_of((jnp.minimum(place, SIDE - 1) * hp + i) * 128, 128)
+                put(i, side_ref[e, pl.ds(row, 128), :])
 
 
 def final_states(doc_lengths, owner_ids, last, side, coming, rows, spread):
     return pl.pallas_call(
         functools.partial(final_kernel, rows),
-        in_specs=[SMEM, SMEM] + [VMEM] * (MEMBERS + 3),
+        in_specs=[SMEM, SMEM] + [VMEM] * (MEMBERS + 2),
         out_specs=VMEM,
-        out_shape=jax.ShapeDtypeStruct((spread,) + coming.shape, BF16),
+        out_shape=jax.ShapeDtypeStruct((spread,) + coming.shape[1:], BF16),
         scratch_shapes=[
             pltpu.VMEM((MEMBERS,) + last[0].shape, BF16),
-            pltpu.VMEM((MEMBERS,) + coming.shape, F32),
+            pltpu.VMEM((MEMBERS,) + coming.shape[1:], F32),
         ],
         compiler_params=SMALL,
         name="final_states",
-    )(doc_lengths, owner_ids, *last, *side, coming)
+    )(doc_lengths, owner_ids, *last, side, coming)
 
 
 def finish_kernel(
@@ -607,41 +605,36 @@
     quads = spread // MEMBERS
     hp = heads // MEMBERS
     near = [[q * MEMBERS + m for m in range(MEMBERS)] for q in range(quads)]
-    onward = [(s, s + MEMBERS) for s in range(spread - MEMBERS)]
+    lines = [[q * MEMBERS + m for q in range(quads)] for m in range(MEMBERS)]
     decay_rows = log_decay.T
     barrier = lax.optimization_barrier
 
-    side1, side2, crow, flags, *last = piece_states(doc_lengths, owner_ids, decay_rows, keys, values)
-    early = functools.partial(early_attention, doc_lengths, queries, keys, values)
+    side, crow, flags, *last = piece_states(doc_lengths, owner_ids, decay_rows, keys, values)
     last = by_distance(last, spread)
-    side1, last[1] = barrier((side1, last[1]))
-    side1 = swap(side1, near)
-    local = early(crow, [], 0)
-    last, local = barrier((last, local))
-
-    coming = []
-    for _ in range(quads - 1):
-        leaving = leave_quad(doc_lengths, last, coming, rows, hp)
-        coming = [lax.ppermute(leaving, "seq", onward)]
-    crow_1, leaving = barrier((crow, leaving))
-    local = early(crow_1, [local], 1)
-    side1, side2, local, flags, gain = barrier((side1, side2, local, flags, gain))
-    side2 = swap(side2, near)
-    gain = gain.reshape(1, -1)
 
     def send_rest():
         rest, _ = piece_states(doc_lengths, owner_ids, decay_rows, keys, values, spread)
         return lax.dynamic_index_in_dim(swap(rest), flags[3], 0, True)
 
+    gain = gain.reshape(1, -1)
     rest = lax.cond(flags[2] > 0, send_rest, lambda: jnp.zeros((1, heads, 128, 128), BF16))
     from_quad = [flags[0] == q for q in range(1, quads)]
-    coming, rest, gain, late, from_quad, local = barrier((coming[0], rest, gain, flags[1] > 0, from_quad, local))
+    last, rest, gain, late, from_quad = barrier((last, rest, gain, flags[1] > 0, from_quad))
+
+    side, last = barrier((side, last))
+    side = swap(side, near)
+    coming = []
+    for q in range(1, quads):
+        leaving = leave_quad(doc_lengths, last, coming, rows, hp)
+        coming = [lax.all_gather(leaving, "seq", axis_index_groups=lines)]
+    crow_1, leaving = barrier((crow, leaving))
+    local = early_attention(doc_lengths, queries, keys, values, crow_1, [], 0)
+    coming, local = barrier((coming[0], local))
 
     entering = by_distance(enter_states(doc_lengths, last, coming, rows), spread)
-    finals = final_states(doc_lengths, owner_ids, last, [side1, side2], coming, rows, spread)
-    entering[1], finals = barrier((entering[1], finals))
+    finals = final_states(doc_lengths, owner_ids, last, side, coming, rows, spread)
+    entering, finals = barrier((entering, finals))
     arrived = swap(finals).reshape(quads, 1, heads, 128, 128)
-    entering, finals = barrier((entering, finals))
     mixed = finish(doc_lengths, queries, keys, values, entering, local, gate, gain, crow)
     owned = arrived[0]
     for q in range(1, quads):

time: 110 us -> 91.6 us (0.83)
  waiting for transfers between devices: 32.2 us -> 11.3 us
  blocking collectives: 0 us -> 18 us
  starting transfers between devices: 32.2 us -> 18.6 us
  Pallas kernels: 39.1 us -> 37.4 us
    ppermute x6, waiting for transfers between devices: 31.5 us -> 6.59 us  [by_distance(): lax.ppermute(parcels[x], 'seq', [(s, s ^ x) for s in range(spread)])]
    all_gather x0 -> x1, blocking collectives: none -> 18 us  [on_device(): coming = [lax.all_gather(leaving, 'seq', axis_index_groups=lines)]]
    all_to_all x3 -> x2, starting transfers between devices: 15.8 us -> 7.51 us  [swap(): lax.all_to_all(x, 'seq', split_axis=0, concat_axis=0, axis_index_groups=g...]
    all_to_all x3 -> x2, waiting for transfers between devices: 0.01 us -> 4.69 us  [swap(): lax.all_to_all(x, 'seq', split_axis=0, concat_axis=0, axis_index_groups=g...]
    ppermute x1 -> x0, starting transfers between devices: 4.45 us -> none  [on_device(): coming = [lax.ppermute(leaving, 'seq', onward)]]
    pallas_call x2 -> x1, Pallas kernels: 10.4 us -> 8.09 us  [early_attention(): pl.pallas_call(functools.partial(early_kernel, skip), grid=(count // 2,),...]
  transfers between devices with their start and end apart: 10 -> 8, of which waited for: 7 -> 5; matrix products, arithmetic and copies ran while one was open for 1% -> 1% of each run, Pallas kernels for 29% -> 32%
where the time goes in v1:
time: 91.6 us; the launch traced here: 91.1 us
  Pallas kernels  37.4 us (41%)
  starting transfers between devices  18.6 us (20%)
  blocking collectives  18 us (20%)
  waiting for transfers between devices  11.3 us (12%)
  between operations  2.78 us (3%)
  local copies, waits for them, and re-layouts  2.04 us (2%)
  other arithmetic  0.92 us (1%)
    all_gather x1, blocking collectives, on_device(): coming = [lax.all_gather(leaving, 'seq', axis_index_groups=lines)]  18 us
    pallas_call x1, Pallas kernels, finish(): pl.pallas_call(finish_kernel, grid=(heads // 2,), in_specs=[SMEM, wide, l...  17.7 us
    ppermute x6, starting transfers between devices, by_distance(): lax.ppermute(parcels[x], 'seq', [(s, s ^ x) for s in range(spread)])  11.1 us
    pallas_call x1, Pallas kernels, early_attention(): pl.pallas_call(functools.partial(early_kernel, skip), grid=(count // 2,),...  8.09 us
    pallas_call x1, Pallas kernels, piece_states(): pl.pallas_call(functools.partial(pieces_kernel, by_owner), grid=(heads //...  7.84 us
    all_to_all x2, starting transfers between devices, swap(): lax.all_to_all(x, 'seq', split_axis=0, concat_axis=0, axis_index_groups=g...  7.51 us
    ppermute x6, waiting for transfers between devices, by_distance(): lax.ppermute(parcels[x], 'seq', [(s, s ^ x) for s in range(spread)])  6.59 us
    all_to_all x2, waiting for transfers between devices, swap(): lax.all_to_all(x, 'seq', split_axis=0, concat_axis=0, axis_index_groups=g...  4.69 us
  transfers between devices with their start and end apart: 8, of which 5 were waited for; matrix products, arithmetic and copies ran while one was open for 1% of the time, Pallas kernels for 32%

profile of v1, /device:TPU:0, one launch (start us, length us, event | category | flops | bytes accessed | tf_op | source)
XLA Modules:
  0.0 91.1 jit_solution(1583300083639586442)
XLA Ops:
  0.6 0.0 copy-start.7
  0.6 0.0 copy-start.2
  0.6 0.0 copy-start.5
  0.7 0.0 copy-start.6
  0.7 7.8 %piece_states.3 = (bf16[4,1536,128]{2,1,0:T(8,128)(2,1)}, f32[16,1024]{1,0:T(8,128)}, s32[4]{0:T(128)S(1)}, bf16[528,128]{1,0:T(8,128)(2,1)}, bf16[528,128]{1,0:...) custom-call(s32[8]{0:T(128)} %len_ref.11, s32[8]{0:T(128)} %own_ref.3, f32[16,1024]{1,0:T(8,128)} %bitcast.12, ...), custom_call_target="tpu_custom_call" | custom-call | flops 1073741824 | bytes 8388608 | tf_op jit(solution)/shard_map/piece_states/pallas_call | solution.py:239
  8.5 3.0 %collective-permute-start = (bf16[528,128]{1,0:T(8,128)(2,1)}, bf16[528,128]{1,0:T(8,128)(2,1)S(1)}, u32[]{:S(2)}, u32[]{:S(2)}) collective-permute-start(bf16[528,128]{1,0:T(8,128)(2,1)} %get-tuple-element.58), channel_id=1, source_target_pairs={{0,2},{2,0},{4,6},{6,4},{8,10},{10,8},{12,14},{14,12},{1,3},{3,1},... | collective-permute-start | bytes 405512 | tf_op jit(solution)/shard_map/ppermute | solution.py:599
  11.5 1.6 %collective-permute-start.1 = (bf16[528,128]{1,0:T(8,128)(2,1)}, bf16[528,128]{1,0:T(8,128)(2,1)S(1)}, u32[]{:S(2)}, u32[]{:S(2)}) collective-permute-start(bf16[528,128]{1,0:T(8,128)(2,1)} %get-tuple-element.59), channel_id=1, source_target_pairs={{0,4},{2,6},{4,0},{6,2},{8,12},{10,14},{12,8},{14,10},{1,5},{3,7},... | collective-permute-start | bytes 405512 | tf_op jit(solution)/shard_map/ppermute | solution.py:599
  13.1 0.0 collective-permute-start.2
  13.1 0.7 fusion
  14.4 0.0 copy-done.7
  14.4 0.6 reshape.42.gain_ref
  16.4 0.0 copy-done.2
  16.4 0.0 copy-done.5
  16.4 0.0 copy-done.6
  16.4 0.0 copy-start
  16.4 0.1 conditional.1
  16.4 0.1 broadcast.12
  16.6 0.0 collective-permute-done.refs_1_
  16.6 1.7 %collective-permute-done.1.refs_2_ = bf16[528,128]{1,0:T(8,128)(2,1)S(1)} collective-permute-done((bf16[528,128]{1,0:T(8,128)(2,1)}, bf16[528,128]{1,0:T(8,128)(2,1)S(1)}, u32[]{:S(2)}, u32[]{:S(2)}) %collective-permute-start.1) | collective-permute-done | bytes 135200 | tf_op jit(solution)/shard_map/ppermute | solution.py:599
  18.3 1.2 %collective-permute-done.2.refs_3_ = bf16[528,128]{1,0:T(8,128)(2,1)S(1)} collective-permute-done((bf16[528,128]{1,0:T(8,128)(2,1)}, bf16[528,128]{1,0:T(8,128)(2,1)S(1)}, u32[]{:S(2)}, u32[]{:S(2)}) %collective-permute-start.2) | collective-permute-done | bytes 135200 | tf_op jit(solution)/shard_map/ppermute | solution.py:599
  19.5 4.0 %all-to-all-start.1 = ((bf16[4,1536,128]{2,1,0:T(8,128)(2,1)}), bf16[4,1536,128]{2,1,0:T(8,128)(2,1)S(1)}, u32[]{:S(2)}, u32[]{:S(2)}) async-start(bf16[4,1536,128]{2,1,0:T(8,128)(2,1)} %get-tuple-element.77), calls=%async_computation.1 | async-start | bytes 3145728 | tf_op jit(solution)/shard_map/all_to_all | solution.py:594
  23.4 0.0 copy-done
  23.5 0.7 leave_quad.1
  24.2 18.0 %all-gather = bf16[8,128,128]{2,1,0:T(8,128)(2,1)S(1)} all-gather(bf16[4,128,128]{2,1,0:T(8,128)(2,1)S(1)} %leave_quad.1), channel_id=2, replica_groups={{0,8},{2,10},{4,12},{6,14},{1,9},{3,11},{5,13},{7,15},{16,24},{18,26},{..., dimensions={0}, use_global_device_ids=true | all-gather | bytes 393216 | tf_op jit(solution)/shard_map/all_gather | solution.py:629
  42.2 8.1 %early_attention.1.local_ref = f32[1024,1024]{1,0:T(8,128)} custom-call(s32[8]{0:T(128)S(1)} %copy-done.5, bf16[1024,2048]{1,0:T(8,128)(2,1)} %q_ref.3, bf16[1024,2048]{1,0:T(8,128)(2,1)} %k_ref.5, bf16[1024,2048]{1,0:T(8,128)(2,1)} %v_ref.5, f32[16,1024]{1,0:T(8,128)} %get-tuple-element.71.crow_ref), custom_call_target="tpu_custom_call" | custom-call | flops 2147483648 | bytes 10485760 | tf_op jit(solution)/shard_map/early_attention/pallas_call | solution.py:362
  50.3 0.8 enter_states.1
  51.1 0.0 copy-start.1
  51.1 0.6 copy-done.1
  51.7 1.7 %collective-permute-start.3 = (bf16[4,128,128]{2,1,0:T(8,128)(2,1)S(1)}, bf16[4,128,128]{2,1,0:T(8,128)(2,1)S(1)}, u32[]{:S(2)}, u32[]{:S(2)}) collective-permute-start(bf16[4,128,128]{2,1,0:T(8,128)(2,1)S(1)} %get-tuple-element.74), channel_id=1, source_target_pairs={{0,2},{2,0},{4,6},{6,4},{8,10},{10,8},{12,14},{14,12},{1,3},{3,1},... | collective-permute-start | bytes 393224 | tf_op jit(solution)/shard_map/ppermute | solution.py:599
  53.4 4.8 %collective-permute-start.4 = (bf16[4,128,128]{2,1,0:T(8,128)(2,1)S(1)}, bf16[4,128,128]{2,1,0:T(8,128)(2,1)S(1)}, u32[]{:S(2)}, u32[]{:S(2)}) collective-permute-start(bf16[4,128,128]{2,1,0:T(8,128)(2,1)S(1)} %get-tuple-element.75), channel_id=1, source_target_pairs={{0,4},{2,6},{4,0},{6,2},{8,12},{10,14},{12,8},{14,10},{1,5},{3,7},... | collective-permute-start | bytes 393224 | tf_op jit(solution)/shard_map/ppermute | solution.py:599
  58.2 0.0 collective-permute-start.5
  58.2 0.0 all-to-all-done.1.refs_4_
  58.2 2.3 %final_states.1 = bf16[8,4,128,128]{3,2,1,0:T(8,128)(2,1)} custom-call(s32[8]{0:T(128)} %len_ref.11, s32[8]{0:T(128)} %own_ref.3, bf16[528,128]{1,0:T(8,128)(2,1)S(1)} %copy-done, bf16[528,128]{1,0:T(8,128)(2,1)S(1)} %collective-permute-done.refs_1_, bf16[528,128]{1,0:T(8,128)(2,1)S(1)} %collective-permute-done.1.refs_2_, ...), custom_call_target="tpu_custom_call" | custom-call | tf_op jit(solution)/shard_map/final_states/pallas_call | solution.py:504
  60.5 0.0 collective-permute-done.3.e1
  60.5 0.0 copy-start.3
  60.5 0.6 collective-permute-done.4.e2
  61.2 0.0 copy-start.4
  61.2 3.0 %collective-permute-done.5.e3 = bf16[4,128,128]{2,1,0:T(8,128)(2,1)} collective-permute-done((bf16[4,128,128]{2,1,0:T(8,128)(2,1)S(1)}, bf16[4,128,128]{2,1,0:T(8,128)(2,1)}, u32[]{:S(2)}, u32[]{:S(2)}) %collective-permute-start.5) | collective-permute-done | bytes 131104 | tf_op jit(solution)/shard_map/ppermute | solution.py:599
  64.2 3.6 %all-to-all-start.2 = ((bf16[8,4,128,128]{3,2,1,0:T(8,128)(2,1)}), bf16[8,4,128,128]{3,2,1,0:T(8,128)(2,1)S(1)}, u32[]{:S(2)}, u32[]{:S(2)}) async-start(bf16[8,4,128,128]{3,2,1,0:T(8,128)(2,1)} %final_states.1), calls=%async_computation.2 | async-start | bytes 2097152 | tf_op jit(solution)/shard_map/all_to_all | solution.py:594
  67.7 0.0 copy-done.3
  67.8 0.0 copy-done.4
  67.8 17.7 %finish.1 = bf16[1024,2048]{1,0:T(8,128)(2,1)} custom-call(s32[8]{0:T(128)} %len_ref.11, bf16[1024,2048]{1,0:T(8,128)(2,1)} %q_ref.3, bf16[1024,2048]{1,0:T(8,128)(2,1)} %k_ref.5, bf16[1024,2048]{1,0:T(8,128)(2,1)} %v_ref.5, bf16[4,128,128]{2,1,0:T(8,128)(2,1)} %copy-done.1, bf16[4,128,128]{2,1,0:T(8,128)(2,1)} %copy-done.3, bf16[4,128,128]{2,1,0:T(8,128)(2,1)} %copy-done.4, ...), custom_call_target="tpu_custom_call" | custom-call | flops 4294967296 | bytes 20971520 | tf_op jit(solution)/shard_map/finish/pallas_call | solution.py:571
  85.4 4.7 %all-to-all-done.2 = bf16[8,4,128,128]{3,2,1,0:T(8,128)(2,1)S(1)} async-done(((bf16[8,4,128,128]{3,2,1,0:T(8,128)(2,1)}), bf16[8,4,128,128]{3,2,1,0:T(8,128)(2,1)S(1)}, u32[]{:S(2)}, u32[]{:S(2)}) %all-to-all-start.2) | async-done | bytes 1048608 | tf_op jit(solution)/shard_map/all_to_all | solution.py:594
  90.1 0.1 slice_select_fusion
  90.2 0.9 bitcast_select_fusion
Async XLA Ops:
  0.6 13.8 %copy-start.7 = (bf16[2048]{0:T(1024)(128)(2,1)S(1)}, bf16[2048]{0:T(1024)(128)(2,1)}, u32[]{:S(2)}) copy-start(bf16[2048]{0:T(1024)(128)(2,1)} %param.15) | copy-start | bytes 12292
  0.6 15.8 %copy-start.2 = (f32[1024,16]{0,1:T(8,128)S(1)}, f32[1024,16]{0,1:T(8,128)}, u32[]{:S(2)}) copy-start(f32[1024,16]{0,1:T(8,128)} %param.13) | copy-start | bytes 196612
  0.6 15.8 %copy-start.5 = (s32[8]{0:T(128)S(1)}, s32[8]{0:T(128)}, u32[]{:S(2)}) copy-start(s32[8]{0:T(128)} %len_ref.11) | copy-start | bytes 100
  0.7 15.8 %copy-start.6 = (s32[8]{0:T(128)S(1)}, s32[8]{0:T(128)}, u32[]{:S(2)}) copy-start(s32[8]{0:T(128)} %own_ref.3) | copy-start | bytes 100
  8.5 8.0 %collective-permute-start = (bf16[528,128]{1,0:T(8,128)(2,1)}, bf16[528,128]{1,0:T(8,128)(2,1)S(1)}, u32[]{:S(2)}, u32[]{:S(2)}) collective-permute-start(bf16[528,128]{1,0:T(8,128)(2,1)} %get-tuple-element.58), channel_id=1, source_target_pairs={{0,2},{2,0},{4,6},{6,4},{8,10},{10,8},{12,14},{14,12},{1,3},{3,1},... | collective-permute-start | bytes 405512 | tf_op jit(solution)/shard_map/ppermute | solution.py:599
  11.5 6.7 %collective-permute-start.1 = (bf16[528,128]{1,0:T(8,128)(2,1)}, bf16[528,128]{1,0:T(8,128)(2,1)S(1)}, u32[]{:S(2)}, u32[]{:S(2)}) collective-permute-start(bf16[528,128]{1,0:T(8,128)(2,1)} %get-tuple-element.59), channel_id=1, source_target_pairs={{0,4},{2,6},{4,0},{6,2},{8,12},{10,14},{12,8},{14,10},{1,5},{3,7},... | collective-permute-start | bytes 405512 | tf_op jit(solution)/shard_map/ppermute | solution.py:599
  13.1 6.4 %collective-permute-start.2 = (bf16[528,128]{1,0:T(8,128)(2,1)}, bf16[528,128]{1,0:T(8,128)(2,1)S(1)}, u32[]{:S(2)}, u32[]{:S(2)}) collective-permute-start(bf16[528,128]{1,0:T(8,128)(2,1)} %get-tuple-element.60), channel_id=1, source_target_pairs={{0,6},{2,4},{4,2},{6,0},{8,14},{10,12},{12,10},{14,8},{1,7},{3,5},... | collective-permute-start | bytes 405512 | tf_op jit(solution)/shard_map/ppermute | solution.py:599
  16.4 7.0 %copy-start = (bf16[528,128]{1,0:T(8,128)(2,1)S(1)}, bf16[528,128]{1,0:T(8,128)(2,1)}, u32[]{:S(2)}) copy-start(bf16[528,128]{1,0:T(8,128)(2,1)} %get-tuple-element.66.refs_0_) | copy-start | bytes 405508
  19.5 38.7 %all-to-all-start.1 = ((bf16[4,1536,128]{2,1,0:T(8,128)(2,1)}), bf16[4,1536,128]{2,1,0:T(8,128)(2,1)S(1)}, u32[]{:S(2)}, u32[]{:S(2)}) async-start(bf16[4,1536,128]{2,1,0:T(8,128)(2,1)} %get-tuple-element.77), calls=%async_computation.1 | async-start | bytes 3145728 | tf_op jit(solution)/shard_map/all_to_all | solution.py:594
  51.1 0.7 copy-start.1
  51.7 8.8 %collective-permute-start.3 = (bf16[4,128,128]{2,1,0:T(8,128)(2,1)S(1)}, bf16[4,128,128]{2,1,0:T(8,128)(2,1)S(1)}, u32[]{:S(2)}, u32[]{:S(2)}) collective-permute-start(bf16[4,128,128]{2,1,0:T(8,128)(2,1)S(1)} %get-tuple-element.74), channel_id=1, source_target_pairs={{0,2},{2,0},{4,6},{6,4},{8,10},{10,8},{12,14},{14,12},{1,3},{3,1},... | collective-permute-start | bytes 393224 | tf_op jit(solution)/shard_map/ppermute | solution.py:599
  53.4 7.7 %collective-permute-start.4 = (bf16[4,128,128]{2,1,0:T(8,128)(2,1)S(1)}, bf16[4,128,128]{2,1,0:T(8,128)(2,1)S(1)}, u32[]{:S(2)}, u32[]{:S(2)}) collective-permute-start(bf16[4,128,128]{2,1,0:T(8,128)(2,1)S(1)} %get-tuple-element.75), channel_id=1, source_target_pairs={{0,4},{2,6},{4,0},{6,2},{8,12},{10,14},{12,8},{14,10},{1,5},{3,7},... | collective-permute-start | bytes 393224 | tf_op jit(solution)/shard_map/ppermute | solution.py:599
  58.2 6.0 %collective-permute-start.5 = (bf16[4,128,128]{2,1,0:T(8,128)(2,1)S(1)}, bf16[4,128,128]{2,1,0:T(8,128)(2,1)}, u32[]{:S(2)}, u32[]{:S(2)}) collective-permute-start(bf16[4,128,128]{2,1,0:T(8,128)(2,1)S(1)} %get-tuple-element.76), channel_id=1, source_target_pairs={{0,6},{2,4},{4,2},{6,0},{8,14},{10,12},{12,10},{14,8},{1,7},{3,5},... | collective-permute-start | bytes 393224 | tf_op jit(solution)/shard_map/ppermute | solution.py:599
  60.5 7.2 %copy-start.3 = (bf16[4,128,128]{2,1,0:T(8,128)(2,1)}, bf16[4,128,128]{2,1,0:T(8,128)(2,1)S(1)}, u32[]{:S(2)}) copy-start(bf16[4,128,128]{2,1,0:T(8,128)(2,1)S(1)} %collective-permute-done.3.e1) | copy-start | bytes 393220
  61.2 6.6 %copy-start.4 = (bf16[4,128,128]{2,1,0:T(8,128)(2,1)}, bf16[4,128,128]{2,1,0:T(8,128)(2,1)S(1)}, u32[]{:S(2)}) copy-start(bf16[4,128,128]{2,1,0:T(8,128)(2,1)S(1)} %collective-permute-done.4.e2) | copy-start | bytes 393220
  64.2 25.9 %all-to-all-start.2 = ((bf16[8,4,128,128]{3,2,1,0:T(8,128)(2,1)}), bf16[8,4,128,128]{3,2,1,0:T(8,128)(2,1)S(1)}, u32[]{:S(2)}, u32[]{:S(2)}) async-start(bf16[8,4,128,128]{3,2,1,0:T(8,128)(2,1)} %final_states.1), calls=%async_computation.2 | async-start | bytes 2097152 | tf_op jit(solution)/shard_map/all_to_all | solution.py:594

commit v2 on v1

--- a/solution.py
+++ b/solution.py
@@ -92,8 +92,8 @@
     return pl.BlockSpec(shape, lambda j: (0,) * len(shape))
 
 
-def pieces_kernel(by_owner, len_ref, own_ref, ld_ref, k_ref, v_ref, *refs):
-    if by_owner:
+def pieces_kernel(rest, len_ref, own_ref, ld_ref, k_ref, v_ref, *refs):
+    if rest:
         side_ref, crow_ref, w_ref, keep_ref = refs
         slots = keep_ref.shape[0]
     else:
@@ -116,12 +116,12 @@
         lows = [jnp.int32(0)] * slots
         highs = [jnp.int32(-1)] * slots
         place, rank, previous = jnp.int32(0), jnp.int32(0), jnp.int32(-1)
-        crowded, owned_in, owned_late = jnp.int32(0), jnp.int32(0), jnp.int32(0)
+        crowded, owned_in = jnp.int32(0), jnp.int32(0)
         for d in range(len(ends)):
             here = (ends[d] > first) & (ends[d] <= last)
             low = jnp.maximum(starts[d] - first, 0)
             for s in range(slots):
-                mine = here & ((place >= SIDE) & (own_ref[d] == s) if by_owner else (place == s))
+                mine = here & (place == s + (SIDE if rest else 0))
                 lows[s] = jnp.where(mine, low, lows[s])
                 highs[s] = jnp.where(mine, ends[d] - 1 - first, highs[s])
             place = place + here.astype(jnp.int32)
@@ -131,13 +131,12 @@
             late = ((rank >= SIDE) & (ends[d] != (device + 1) * rows)).astype(jnp.int32)
             crowded = jnp.maximum(crowded, late)
             owned_in = jnp.where(own_ref[d] == me, device, owned_in)
-            owned_late = jnp.where(own_ref[d] == me, late, owned_late)
         at = iota((heads, rows), 1)
         cum = crow_ref[...]
         total = jnp.zeros((heads, rows), F32)
         for s in range(slots):
             total = total + span_weights(cum, at, lows[s], highs[s])
-        if by_owner:
+        if rest:
             row_at = iota((16, rows), 1)
             for s in range(slots):
                 inside = (row_at >= lows[s]) & (row_at <= highs[s])
@@ -145,9 +144,7 @@
         else:
             total = total + span_weights(cum, at, jnp.maximum(run_start(ends, last) - first, 0), rows - 1)
             flag_ref[0] = owned_in // MEMBERS
-            flag_ref[1] = owned_late
-            flag_ref[2] = crowded
-            flag_ref[3] = owned_in
+            flag_ref[1] = crowded
             high = jnp.int32(-1)
             for s in range(slots):
                 high = jnp.maximum(high, highs[s])
@@ -160,12 +157,15 @@
     def own(states, j):
         return states[j * 128 : (j + 1) * 128, j * 128 : (j + 1) * 128]
 
-    if by_owner:
-        weighted = weigh(k_ref[...].T, w_ref, step * hp).reshape(16, 16, rows)
-        for s in range(slots):
-            states = dot((weighted * keep_ref[s][None]).reshape(256, rows), v_ref[...])
-            for j in range(2):
-                side_ref[s, j] = own(states, j).astype(BF16)
+    if rest:
+        for i in range(0, hp, 2):
+            lanes = slice(i * 128, (i + 2) * 128)
+            weighted = weigh(k_ref[:, lanes].T, w_ref, step * hp + i).reshape(16, 16, rows)
+            for s in range(slots):
+                states = dot((weighted * keep_ref[s][None]).reshape(256, rows), v_ref[:, lanes])
+                for j in range(2):
+                    at = (s * hp + i + j) * 128
+                    side_ref[0, at : at + 128, :] = own(states, j).astype(BF16)
         return
 
     pairs = range(0, hp, 2)
@@ -210,26 +210,22 @@
             last_ref[hp * 128 :, :] = tail
 
 
-def piece_states(doc_lengths, owner_ids, decay_rows, keys, values, spread=0):
+def piece_states(doc_lengths, owner_ids, decay_rows, keys, values, slots):
     heads, rows = decay_rows.shape
-    by_owner = spread > 0
-    hp = 2 if by_owner else heads // MEMBERS
+    rest = slots > SIDE
+    count = slots - SIDE if rest else slots
+    hp = heads // MEMBERS
     wide = pl.BlockSpec((rows, hp * 128), lambda j: (0, j))
+    side = (count * hp * 128, 128)
+    shapes = [jax.ShapeDtypeStruct((MEMBERS,) + side, BF16), jax.ShapeDtypeStruct((heads, rows), F32)]
+    specs = [pl.BlockSpec((1,) + side, lambda j: (j, 0, 0)), whole((heads, rows))]
     scratch = [pltpu.VMEM((heads, rows), F32)]
-    if by_owner:
-        shapes = [jax.ShapeDtypeStruct((spread, heads, 128, 128), BF16), jax.ShapeDtypeStruct((heads, rows), F32)]
-        specs = [pl.BlockSpec((spread, hp, 128, 128), lambda j: (0, j, 0, 0)), whole((heads, rows))]
-        scratch.append(pltpu.VMEM((spread, 16, rows), BF16))
+    if rest:
+        scratch.append(pltpu.VMEM((count, 16, rows), BF16))
     else:
         last = (hp * 128 + EXTRA, 128)
-        shapes = [
-            jax.ShapeDtypeStruct((MEMBERS, SIDE * hp * 128, 128), BF16),
-            jax.ShapeDtypeStruct((heads, rows), F32),
-            jax.ShapeDtypeStruct((4,), jnp.int32),
-            *[jax.ShapeDtypeStruct(last, BF16)] * MEMBERS,
-        ]
-        specs = [pl.BlockSpec((1, SIDE * hp * 128, 128), lambda j: (j, 0, 0)), whole((heads, rows)), SMEM]
-        specs += [whole(last)] * MEMBERS
+        shapes += [jax.ShapeDtypeStruct((2,), jnp.int32)] + [jax.ShapeDtypeStruct(last, BF16)] * MEMBERS
+        specs += [SMEM] + [whole(last)] * MEMBERS
         scratch += [
             pltpu.VMEM((heads, 128), F32),
             pltpu.SMEM((SIDE,), jnp.int32),
@@ -237,8 +233,8 @@
             pltpu.VMEM((rows // TILE, hp, 128, 128), F32),
         ]
     return pl.pallas_call(
-        functools.partial(pieces_kernel, by_owner),
-        grid=(heads // hp,),
+        functools.partial(pieces_kernel, rest),
+        grid=(MEMBERS,),
         in_specs=[SMEM, SMEM, whole((heads, rows)), wide, wide],
         out_specs=specs,
         out_shape=shapes,
@@ -375,11 +371,6 @@
     )(doc_lengths, queries, keys, values, crow, *before)
 
 
-def from_before(in_ref, i):
-    quad = lax.axis_index("seq") // MEMBERS
-    return in_ref[jnp.maximum(quad - 1, 0), i].astype(F32) * (quad > 0).astype(F32)
-
-
 def gather_last(refs, last_ref):
     me = lax.axis_index("seq") % MEMBERS
     for x, ref in enumerate(refs):
@@ -414,7 +405,7 @@
     for i in range(hp):
         state = jnp.zeros((128, 128), F32)
         if len(refs) > MEMBERS + 2:
-            state = from_before(refs[MEMBERS], i)
+            state = refs[MEMBERS][i].astype(F32)
         state = scan_quad(rows, len_ref, last_ref, state, i, hp, lambda e, x: None)
         out_ref[i] = state.astype(BF16)
 
@@ -434,13 +425,13 @@
 def enter_kernel(rows, len_ref, *refs):
     in_ref, out_refs, last_ref, state_ref = refs[MEMBERS], refs[MEMBERS + 1 : -2], refs[-2], refs[-1]
     gather_last(refs[:MEMBERS], last_ref)
-    hp = in_ref.shape[1]
+    hp = in_ref.shape[0]
 
     def note(i, e, state):
         state_ref[e, i] = state
 
     for i in range(hp):
-        scan_quad(rows, len_ref, last_ref, from_before(in_ref, i), i, hp, functools.partial(note, i))
+        scan_quad(rows, len_ref, last_ref, in_ref[i].astype(F32), i, hp, functools.partial(note, i))
     me = lax.axis_index("seq") % MEMBERS
     for x, out_ref in enumerate(out_refs):
         out_ref[...] = state_ref[me ^ x].astype(BF16)
@@ -451,10 +442,10 @@
         functools.partial(enter_kernel, rows),
         in_specs=[SMEM] + [VMEM] * (MEMBERS + 1),
         out_specs=[VMEM] * MEMBERS,
-        out_shape=[jax.ShapeDtypeStruct(coming.shape[1:], BF16)] * MEMBERS,
+        out_shape=[jax.ShapeDtypeStruct(coming.shape, BF16)] * MEMBERS,
         scratch_shapes=[
             pltpu.VMEM((MEMBERS,) + last[0].shape, BF16),
-            pltpu.VMEM((MEMBERS,) + coming.shape[1:], F32),
+            pltpu.VMEM((MEMBERS,) + coming.shape, F32),
         ],
         compiler_params=SMALL,
         name="enter_states",
@@ -462,9 +453,9 @@
 
 
 def final_kernel(rows, len_ref, own_ref, *refs):
-    side_ref, in_ref, out_ref, last_ref, state_ref = refs[MEMBERS:]
+    side_ref, rest_ref, in_ref, out_ref, last_ref, state_ref, piece_ref = refs[MEMBERS:]
     gather_last(refs[:MEMBERS], last_ref)
-    hp = in_ref.shape[1]
+    hp = in_ref.shape[0]
     ends = read_ends(len_ref, len_ref.shape[0])
     base = lax.axis_index("seq") // MEMBERS * MEMBERS
 
@@ -472,7 +463,7 @@
         state_ref[e, i] = state
 
     for i in range(hp):
-        scan_quad(rows, len_ref, last_ref, from_before(in_ref, i), i, hp, functools.partial(note, i))
+        scan_quad(rows, len_ref, last_ref, in_ref[i].astype(F32), i, hp, functools.partial(note, i))
     out_ref[...] = jnp.zeros_like(out_ref)
     place, previous = jnp.int32(0), jnp.int32(-1)
     for d in range(len(ends)):
@@ -493,26 +484,33 @@
             for i in range(hp):
                 put(i, last_ref[e, i * 128 : (i + 1) * 128, :])
 
-        @pl.when(mine & jnp.logical_not(at_end))
+        @pl.when(mine & jnp.logical_not(at_end) & (place < SIDE))
         def _():
             for i in range(hp):
-                row = pl.multiple_of((jnp.minimum(place, SIDE - 1) * hp + i) * 128, 128)
-                put(i, side_ref[e, pl.ds(row, 128), :])
-
-
-def final_states(doc_lengths, owner_ids, last, side, coming, rows, spread):
+                put(i, side_ref[e, pl.ds(pl.multiple_of((place * hp + i) * 128, 128), 128), :])
+
+        @pl.when(mine & jnp.logical_not(at_end) & (place >= SIDE))
+        def _():
+            for i in range(hp):
+                row = pl.multiple_of(((place - SIDE) * hp + i) * 128, 128)
+                pltpu.sync_copy(rest_ref.at[e, pl.ds(row, 128), :], piece_ref)
+                put(i, piece_ref[...])
+
+
+def final_states(doc_lengths, owner_ids, last, side, rest, coming, rows, spread):
     return pl.pallas_call(
         functools.partial(final_kernel, rows),
-        in_specs=[SMEM, SMEM] + [VMEM] * (MEMBERS + 2),
+        in_specs=[SMEM, SMEM] + [VMEM] * (MEMBERS + 1) + [pl.BlockSpec(memory_space=pl.ANY), VMEM],
         out_specs=VMEM,
-        out_shape=jax.ShapeDtypeStruct((spread,) + coming.shape[1:], BF16),
+        out_shape=jax.ShapeDtypeStruct((spread,) + coming.shape, BF16),
         scratch_shapes=[
             pltpu.VMEM((MEMBERS,) + last[0].shape, BF16),
-            pltpu.VMEM((MEMBERS,) + coming.shape[1:], F32),
+            pltpu.VMEM((MEMBERS,) + coming.shape, F32),
+            pltpu.VMEM((128, 128), BF16),
         ],
         compiler_params=SMALL,
         name="final_states",
-    )(doc_lengths, owner_ids, *last, side, coming)
+    )(doc_lengths, owner_ids, *last, side, rest, coming)
 
 
 def finish_kernel(
@@ -605,41 +603,42 @@
     quads = spread // MEMBERS
     hp = heads // MEMBERS
     near = [[q * MEMBERS + m for m in range(MEMBERS)] for q in range(quads)]
-    lines = [[q * MEMBERS + m for q in range(quads)] for m in range(MEMBERS)]
+    onward = [(s, s + MEMBERS) for s in range(spread - MEMBERS)]
     decay_rows = log_decay.T
     barrier = lax.optimization_barrier
 
-    side, crow, flags, *last = piece_states(doc_lengths, owner_ids, decay_rows, keys, values)
+    side, crow, flags, *last = piece_states(doc_lengths, owner_ids, decay_rows, keys, values, SIDE)
     last = by_distance(last, spread)
+    gain = gain.reshape(1, -1)
+    crowded = flags[1] > 0
+    from_quad = [flags[0] == q for q in range(1, quads)]
+    slots = max(doc_lengths.shape[0] - 1, SIDE + 1)
 
     def send_rest():
-        rest, _ = piece_states(doc_lengths, owner_ids, decay_rows, keys, values, spread)
-        return lax.dynamic_index_in_dim(swap(rest), flags[3], 0, True)
-
-    gain = gain.reshape(1, -1)
-    rest = lax.cond(flags[2] > 0, send_rest, lambda: jnp.zeros((1, heads, 128, 128), BF16))
-    from_quad = [flags[0] == q for q in range(1, quads)]
-    last, rest, gain, late, from_quad = barrier((last, rest, gain, flags[1] > 0, from_quad))
-
-    side, last = barrier((side, last))
+        return swap(piece_states(doc_lengths, owner_ids, decay_rows, keys, values, slots)[0], near)
+
+    none = jnp.zeros((MEMBERS, (slots - SIDE) * hp * 128, 128), BF16)
+    rest = lax.cond(crowded, send_rest, lambda: none)
+    last, side, gain, rest, from_quad = barrier((last, side, gain, rest, from_quad))
+
     side = swap(side, near)
     coming = []
-    for q in range(1, quads):
+    for _ in range(quads - 1):
         leaving = leave_quad(doc_lengths, last, coming, rows, hp)
-        coming = [lax.all_gather(leaving, "seq", axis_index_groups=lines)]
+        coming = [lax.ppermute(leaving, "seq", onward)]
     crow_1, leaving = barrier((crow, leaving))
     local = early_attention(doc_lengths, queries, keys, values, crow_1, [], 0)
-    coming, local = barrier((coming[0], local))
+    coming, local, side = barrier((coming[0], local, side))
 
     entering = by_distance(enter_states(doc_lengths, last, coming, rows), spread)
-    finals = final_states(doc_lengths, owner_ids, last, side, coming, rows, spread)
+    finals = final_states(doc_lengths, owner_ids, last, side, rest, coming, rows, spread)
     entering, finals = barrier((entering, finals))
     arrived = swap(finals).reshape(quads, 1, heads, 128, 128)
     mixed = finish(doc_lengths, queries, keys, values, entering, local, gate, gain, crow)
     owned = arrived[0]
     for q in range(1, quads):
         owned = jnp.where(from_quad[q - 1], arrived[q], owned)
-    return mixed, jnp.where(late, rest, owned)
+    return mixed, owned
 
 
 def solution(mesh):

time: 91.6 us -> 82.2 us (0.90)
  blocking collectives: 18 us -> 0 us
  waiting for transfers between devices: 11.3 us -> 16.1 us
  starting transfers between devices: 18.6 us -> 23 us
    all_gather x1 -> x0, blocking collectives: 18 us -> none  [on_device(): coming = [lax.all_gather(leaving, 'seq', axis_index_groups=lines)]]
    ppermute x0 -> x1, waiting for transfers between devices: none -> 5.5 us  [on_device(): coming = [lax.ppermute(leaving, 'seq', onward)]]
    ppermute x0 -> x1, starting transfers between devices: none -> 4.5 us  [on_device(): coming = [lax.ppermute(leaving, 'seq', onward)]]
    ppermute x6, starting transfers between devices: 11.1 us -> 8.17 us  [by_distance(): lax.ppermute(parcels[x], 'seq', [(s, s ^ x) for s in range(spread)])]
    all_to_all x2, starting transfers between devices: 7.51 us -> 10.3 us  [swap(): lax.all_to_all(x, 'seq', split_axis=0, concat_axis=0, axis_index_groups=g...]
    ppermute x6, waiting for transfers between devices: 6.59 us -> 5.66 us  [by_distance(): lax.ppermute(parcels[x], 'seq', [(s, s ^ x) for s in range(spread)])]
  transfers between devices with their start and end apart: 8 -> 9, of which waited for: 5 -> 7; matrix products, arithmetic and copies ran while one was open for 1% -> 3% of each run, Pallas kernels for 32% -> 35%
where the time goes in v2:
time: 82.2 us; the launch traced here: 81.7 us
  Pallas kernels  37.4 us (45%)
  starting transfers between devices  23 us (28%)
  waiting for transfers between devices  16.1 us (20%)
  local copies, waits for them, and re-layouts  2.29 us (3%)
  between operations  2.03 us (2%)
  other arithmetic  0.85 us (1%)
    pallas_call x1, Pallas kernels, finish(): pl.pallas_call(finish_kernel, grid=(heads // 2,), in_specs=[SMEM, wide, l...  17.7 us
    all_to_all x2, starting transfers between devices, swap(): lax.all_to_all(x, 'seq', split_axis=0, concat_axis=0, axis_index_groups=g...  10.3 us
    ppermute x6, starting transfers between devices, by_distance(): lax.ppermute(parcels[x], 'seq', [(s, s ^ x) for s in range(spread)])  8.17 us
    pallas_call x1, Pallas kernels, early_attention(): pl.pallas_call(functools.partial(early_kernel, skip), grid=(count // 2,),...  8.08 us
    pallas_call x1, Pallas kernels, piece_states(): pl.pallas_call(functools.partial(pieces_kernel, rest), grid=(MEMBERS,), i...  7.84 us
    ppermute x6, waiting for transfers between devices, by_distance(): lax.ppermute(parcels[x], 'seq', [(s, s ^ x) for s in range(spread)])  5.66 us
    ppermute x1, waiting for transfers between devices, on_device(): coming = [lax.ppermute(leaving, 'seq', onward)]  5.5 us
    all_to_all x2, waiting for transfers between devices, swap(): lax.all_to_all(x, 'seq', split_axis=0, concat_axis=0, axis_index_groups=g...  4.97 us
  transfers between devices with their start and end apart: 9, of which 7 were waited for; matrix products, arithmetic and copies ran while one was open for 3% of the time, Pallas kernels for 35%

profile of v2, /device:TPU:0, one launch (start us, length us, event | category | flops | bytes accessed | tf_op | source)
XLA Modules:
  0.0 81.7 jit_solution(17501347532539542144)
XLA Ops:
  0.6 0.0 copy-start.9
  0.6 0.0 copy-start.3
  0.7 0.0 copy-start.7
  0.7 0.0 copy-start.8
  0.7 7.8 %piece_states.3 = (bf16[4,1536,128]{2,1,0:T(8,128)(2,1)}, f32[16,1024]{1,0:T(8,128)}, s32[2]{0:T(128)}, bf16[528,128]{1,0:T(8,128)(2,1)}, bf16[528,128]{1,0:T(8,...) custom-call(s32[8]{0:T(128)} %len_ref.11, s32[8]{0:T(128)} %own_ref.3, f32[16,1024]{1,0:T(8,128)} %bitcast.5, ...), custom_call_target="tpu_custom_call" | custom-call | flops 1073741824 | bytes 8388608 | tf_op jit(solution)/shard_map/piece_states/pallas_call | solution.py:235
  8.5 3.0 %collective-permute-start = (bf16[528,128]{1,0:T(8,128)(2,1)}, bf16[528,128]{1,0:T(8,128)(2,1)S(1)}, u32[]{:S(2)}, u32[]{:S(2)}) collective-permute-start(bf16[528,128]{1,0:T(8,128)(2,1)} %get-tuple-element.50), channel_id=1, source_target_pairs={{0,2},{2,0},{4,6},{6,4},{8,10},{10,8},{12,14},{14,12},{1,3},{3,1},... | collective-permute-start | bytes 405512 | tf_op jit(solution)/shard_map/ppermute | solution.py:597
  11.6 1.6 %collective-permute-start.1 = (bf16[528,128]{1,0:T(8,128)(2,1)}, bf16[528,128]{1,0:T(8,128)(2,1)S(1)}, u32[]{:S(2)}, u32[]{:S(2)}) collective-permute-start(bf16[528,128]{1,0:T(8,128)(2,1)} %get-tuple-element.51), channel_id=1, source_target_pairs={{0,4},{2,6},{4,0},{6,2},{8,12},{10,14},{12,8},{14,10},{1,5},{3,7},... | collective-permute-start | bytes 405512 | tf_op jit(solution)/shard_map/ppermute | solution.py:597
  13.1 0.0 collective-permute-start.2
  13.1 0.0 copy-done.9
  13.1 0.6 reshape.40.gain_ref
  13.7 1.4 %fusion = (s32[1]{0:T(128)}, s32[1]{0:T(128)}) fusion(s32[2]{0:T(128)} %get-tuple-element.54), kind=kLoop, calls=%fused_computation.1 | loop fusion | bytes 16 | tf_op jit(solution)/shard_map/slice | solution.py:614
  16.3 0.0 copy-done.3
  16.4 0.0 copy-done.7
  16.4 0.0 copy-done.8
  16.4 0.0 copy-start
  16.4 0.3 conditional.1
  16.4 0.3 broadcast_in_dim.2
  16.7 0.0 copy-start.2
  16.7 0.0 collective-permute-done.refs_1_
  16.7 1.6 %collective-permute-done.1.refs_2_ = bf16[528,128]{1,0:T(8,128)(2,1)S(1)} collective-permute-done((bf16[528,128]{1,0:T(8,128)(2,1)}, bf16[528,128]{1,0:T(8,128)(2,1)S(1)}, u32[]{:S(2)}, u32[]{:S(2)}) %collective-permute-start.1) | collective-permute-done | bytes 135200 | tf_op jit(solution)/shard_map/ppermute | solution.py:597
  18.3 1.3 %collective-permute-done.2.refs_3_ = bf16[528,128]{1,0:T(8,128)(2,1)S(1)} collective-permute-done((bf16[528,128]{1,0:T(8,128)(2,1)}, bf16[528,128]{1,0:T(8,128)(2,1)S(1)}, u32[]{:S(2)}, u32[]{:S(2)}) %collective-permute-start.2) | collective-permute-done | bytes 135200 | tf_op jit(solution)/shard_map/ppermute | solution.py:597
  19.5 0.0 copy-done.2
  19.5 3.9 %all-to-all-start.1 = ((bf16[4,1536,128]{2,1,0:T(8,128)(2,1)}), bf16[4,1536,128]{2,1,0:T(8,128)(2,1)S(1)}, u32[]{:S(2)}, u32[]{:S(2)}) async-start(bf16[4,1536,128]{2,1,0:T(8,128)(2,1)} %get-tuple-element.61), calls=%async_computation.1 | async-start | bytes 3145728 | tf_op jit(solution)/shard_map/all_to_all | solution.py:592
  23.5 0.0 copy-done
  23.5 0.7 leave_quad.1
  24.2 4.5 %collective-permute-start.3 = (bf16[4,128,128]{2,1,0:T(8,128)(2,1)S(1)}, bf16[4,128,128]{2,1,0:T(8,128)(2,1)S(1)}, u32[]{:S(2)}, u32[]{:S(2)}) collective-permute-start(bf16[4,128,128]{2,1,0:T(8,128)(2,1)S(1)} %leave_quad.1), channel_id=1, source_target_pairs={{0,8},{2,10},{4,12},{6,14},{1,9},{3,11},{5,13},{7,15},{16,24},{18,... | collective-permute-start | bytes 393224 | tf_op jit(solution)/shard_map/ppermute | solution.py:628
  28.7 8.1 %early_attention.1.local_ref = f32[1024,1024]{1,0:T(8,128)} custom-call(s32[8]{0:T(128)S(1)} %copy-done.7, bf16[1024,2048]{1,0:T(8,128)(2,1)} %q_ref.3, bf16[1024,2048]{1,0:T(8,128)(2,1)} %k_ref.5, bf16[1024,2048]{1,0:T(8,128)(2,1)} %v_ref.5, f32[16,1024]{1,0:T(8,128)} %get-tuple-element.60.crow_ref), custom_call_target="tpu_custom_call" | custom-call | flops 2147483648 | bytes 10485760 | tf_op jit(solution)/shard_map/early_attention/pallas_call | solution.py:358
  36.8 5.5 %collective-permute-done.3.refs_4_.refs_6_ = bf16[4,128,128]{2,1,0:T(8,128)(2,1)S(1)} collective-permute-done((bf16[4,128,128]{2,1,0:T(8,128)(2,1)S(1)}, bf16[4,128,128]{2,1,0:T(8,128)(2,1)S(1)}, u32[]{:S(2)}, u32[]{:S(2)}) %collective-permute-start.3) | collective-permute-done | bytes 131104 | tf_op jit(solution)/shard_map/ppermute | solution.py:628
  42.3 0.0 all-to-all-done.1.refs_4_
  42.3 0.8 enter_states.1
  43.1 0.0 copy-start.1
  43.1 1.8 %collective-permute-start.4 = (bf16[4,128,128]{2,1,0:T(8,128)(2,1)S(1)}, bf16[4,128,128]{2,1,0:T(8,128)(2,1)S(1)}, u32[]{:S(2)}, u32[]{:S(2)}) collective-permute-start(bf16[4,128,128]{2,1,0:T(8,128)(2,1)S(1)} %get-tuple-element.64), channel_id=1, source_target_pairs={{0,2},{2,0},{4,6},{6,4},{8,10},{10,8},{12,14},{14,12},{1,3},{3,1},... | collective-permute-start | bytes 393224 | tf_op jit(solution)/shard_map/ppermute | solution.py:597
  44.8 1.1 %collective-permute-start.5 = (bf16[4,128,128]{2,1,0:T(8,128)(2,1)S(1)}, bf16[4,128,128]{2,1,0:T(8,128)(2,1)S(1)}, u32[]{:S(2)}, u32[]{:S(2)}) collective-permute-start(bf16[4,128,128]{2,1,0:T(8,128)(2,1)S(1)} %get-tuple-element.65), channel_id=1, source_target_pairs={{0,4},{2,6},{4,0},{6,2},{8,12},{10,14},{12,8},{14,10},{1,5},{3,7},... | collective-permute-start | bytes 393224 | tf_op jit(solution)/shard_map/ppermute | solution.py:597
  45.9 0.7 collective-permute-start.6
  46.6 2.3 %final_states.1 = bf16[8,4,128,128]{3,2,1,0:T(8,128)(2,1)} custom-call(s32[8]{0:T(128)S(1)} %copy-done.7, s32[8]{0:T(128)S(1)} %copy-done.8, bf16[528,128]{1,0:T(8,128)(2,1)S(1)} %copy-done, bf16[528,128]{1,0:T(8,128)(2,1)S(1)} %collective-permute-done.refs_1_, bf16[528,128]{1,0:T(8,128)(2,1)S(1)} %collective-permute-done.1.refs_2_, ...), custom_call_target="tpu_custom_call" | custom-call | tf_op jit(solution)/shard_map/final_states/pallas_call | solution.py:501
  48.9 0.0 copy-done.1
  48.9 0.6 collective-permute-done.4.e1
  49.5 0.0 copy-start.4
  49.5 0.8 collective-permute-done.5.e2
  50.3 0.0 copy-start.5
  50.3 1.5 %collective-permute-done.6.e3 = bf16[4,128,128]{2,1,0:T(8,128)(2,1)S(1)} collective-permute-done((bf16[4,128,128]{2,1,0:T(8,128)(2,1)S(1)}, bf16[4,128,128]{2,1,0:T(8,128)(2,1)S(1)}, u32[]{:S(2)}, u32[]{:S(2)}) %collective-permute-start.6) | collective-permute-done | bytes 131104 | tf_op jit(solution)/shard_map/ppermute | solution.py:597
  51.8 6.4 %all-to-all-start.2 = ((bf16[8,4,128,128]{3,2,1,0:T(8,128)(2,1)}), bf16[8,4,128,128]{3,2,1,0:T(8,128)(2,1)S(1)}, u32[]{:S(2)}, u32[]{:S(2)}) async-start(bf16[8,4,128,128]{3,2,1,0:T(8,128)(2,1)} %final_states.1), calls=%async_computation.2 | async-start | bytes 2097152 | tf_op jit(solution)/shard_map/all_to_all | solution.py:592
  58.2 0.0 copy-done.4
  58.2 0.0 copy-done.5
  58.2 0.0 copy-done.6
  58.2 17.7 %finish.1 = bf16[1024,2048]{1,0:T(8,128)(2,1)} custom-call(s32[8]{0:T(128)S(1)} %copy-done.7, bf16[1024,2048]{1,0:T(8,128)(2,1)} %q_ref.3, bf16[1024,2048]{1,0:T(8,128)(2,1)} %k_ref.5, bf16[1024,2048]{1,0:T(8,128)(2,1)} %v_ref.5, bf16[4,128,128]{2,1,0:T(8,128)(2,1)} %copy-done.1, bf16[4,128,128]{2,1,0:T(8,128)(2,1)} %copy-done.4, ...), custom_call_target="tpu_custom_call" | custom-call | flops 4294967296 | bytes 20971520 | tf_op jit(solution)/shard_map/finish/pallas_call | solution.py:569
  75.9 5.0 %all-to-all-done.2 = bf16[8,4,128,128]{3,2,1,0:T(8,128)(2,1)S(1)} async-done(((bf16[8,4,128,128]{3,2,1,0:T(8,128)(2,1)}), bf16[8,4,128,128]{3,2,1,0:T(8,128)(2,1)S(1)}, u32[]{:S(2)}, u32[]{:S(2)}) %all-to-all-start.2) | async-done | bytes 1048608 | tf_op jit(solution)/shard_map/all_to_all | solution.py:592
  80.8 0.8 %slice_select_fusion = bf16[4,4,128,128]{3,2,1,0:T(8,128)(2,1)} fusion(bf16[8,4,128,128]{3,2,1,0:T(8,128)(2,1)S(1)} %all-to-all-done.2, pred[]{:T(512)} %bitcast.2), kind=kLoop, calls=%fused_computation | loop fusion | flops 262144 | bytes 1572865 | tf_op jit(solution)/shard_map/jit(_where)/select_n | solution.py:640
  (1 shorter events, 0.0 us)
Async XLA Ops:
  0.6 12.5 %copy-start.9 = (bf16[2048]{0:T(1024)(128)(2,1)S(1)}, bf16[2048]{0:T(1024)(128)(2,1)}, u32[]{:S(2)}) copy-start(bf16[2048]{0:T(1024)(128)(2,1)} %param.15) | copy-start | bytes 12292
  0.6 15.7 %copy-start.3 = (f32[1024,16]{0,1:T(8,128)S(1)}, f32[1024,16]{0,1:T(8,128)}, u32[]{:S(2)}) copy-start(f32[1024,16]{0,1:T(8,128)} %param.13) | copy-start | bytes 196612
  0.7 15.7 %copy-start.7 = (s32[8]{0:T(128)S(1)}, s32[8]{0:T(128)}, u32[]{:S(2)}) copy-start(s32[8]{0:T(128)} %len_ref.11) | copy-start | bytes 100
  0.7 15.7 %copy-start.8 = (s32[8]{0:T(128)S(1)}, s32[8]{0:T(128)}, u32[]{:S(2)}) copy-start(s32[8]{0:T(128)} %own_ref.3) | copy-start | bytes 100
  8.5 8.2 %collective-permute-start = (bf16[528,128]{1,0:T(8,128)(2,1)}, bf16[528,128]{1,0:T(8,128)(2,1)S(1)}, u32[]{:S(2)}, u32[]{:S(2)}) collective-permute-start(bf16[528,128]{1,0:T(8,128)(2,1)} %get-tuple-element.50), channel_id=1, source_target_pairs={{0,2},{2,0},{4,6},{6,4},{8,10},{10,8},{12,14},{14,12},{1,3},{3,1},... | collective-permute-start | bytes 405512 | tf_op jit(solution)/shard_map/ppermute | solution.py:597
  11.6 6.7 %collective-permute-start.1 = (bf16[528,128]{1,0:T(8,128)(2,1)}, bf16[528,128]{1,0:T(8,128)(2,1)S(1)}, u32[]{:S(2)}, u32[]{:S(2)}) collective-permute-start(bf16[528,128]{1,0:T(8,128)(2,1)} %get-tuple-element.51), channel_id=1, source_target_pairs={{0,4},{2,6},{4,0},{6,2},{8,12},{10,14},{12,8},{14,10},{1,5},{3,7},... | collective-permute-start | bytes 405512 | tf_op jit(solution)/shard_map/ppermute | solution.py:597
  13.1 6.4 %collective-permute-start.2 = (bf16[528,128]{1,0:T(8,128)(2,1)}, bf16[528,128]{1,0:T(8,128)(2,1)S(1)}, u32[]{:S(2)}, u32[]{:S(2)}) collective-permute-start(bf16[528,128]{1,0:T(8,128)(2,1)} %get-tuple-element.52), channel_id=1, source_target_pairs={{0,6},{2,4},{4,2},{6,0},{8,14},{10,12},{12,10},{14,8},{1,7},{3,5},... | collective-permute-start | bytes 405512 | tf_op jit(solution)/shard_map/ppermute | solution.py:597
  16.4 7.1 %copy-start = (bf16[528,128]{1,0:T(8,128)(2,1)S(1)}, bf16[528,128]{1,0:T(8,128)(2,1)}, u32[]{:S(2)}) copy-start(bf16[528,128]{1,0:T(8,128)(2,1)} %get-tuple-element.55.refs_0_) | copy-start | bytes 405508
  16.7 2.8 %copy-start.2 = (bf16[4,2048,128]{2,1,0:T(8,128)(2,1)}, bf16[4,2048,128]{2,1,0:T(8,128)(2,1)S(1)}, u32[]{:S(2)}) copy-start(bf16[4,2048,128]{2,1,0:T(8,128)(2,1)S(1)} %get-tuple-element.79.refs_5_) | copy-start | bytes 6291460
  19.5 22.7 %all-to-all-start.1 = ((bf16[4,1536,128]{2,1,0:T(8,128)(2,1)}), bf16[4,1536,128]{2,1,0:T(8,128)(2,1)S(1)}, u32[]{:S(2)}, u32[]{:S(2)}) async-start(bf16[4,1536,128]{2,1,0:T(8,128)(2,1)} %get-tuple-element.61), calls=%async_computation.1 | async-start | bytes 3145728 | tf_op jit(solution)/shard_map/all_to_all | solution.py:592
  24.2 18.1 %collective-permute-start.3 = (bf16[4,128,128]{2,1,0:T(8,128)(2,1)S(1)}, bf16[4,128,128]{2,1,0:T(8,128)(2,1)S(1)}, u32[]{:S(2)}, u32[]{:S(2)}) collective-permute-start(bf16[4,128,128]{2,1,0:T(8,128)(2,1)S(1)} %leave_quad.1), channel_id=1, source_target_pairs={{0,8},{2,10},{4,12},{6,14},{1,9},{3,11},{5,13},{7,15},{16,24},{18,... | collective-permute-start | bytes 393224 | tf_op jit(solution)/shard_map/ppermute | solution.py:628
  43.1 5.9 %copy-start.1 = (bf16[4,128,128]{2,1,0:T(8,128)(2,1)}, bf16[4,128,128]{2,1,0:T(8,128)(2,1)S(1)}, u32[]{:S(2)}) copy-start(bf16[4,128,128]{2,1,0:T(8,128)(2,1)S(1)} %get-tuple-element.69.e0) | copy-start | bytes 393220
  43.1 6.4 %collective-permute-start.4 = (bf16[4,128,128]{2,1,0:T(8,128)(2,1)S(1)}, bf16[4,128,128]{2,1,0:T(8,128)(2,1)S(1)}, u32[]{:S(2)}, u32[]{:S(2)}) collective-permute-start(bf16[4,128,128]{2,1,0:T(8,128)(2,1)S(1)} %get-tuple-element.64), channel_id=1, source_target_pairs={{0,2},{2,0},{4,6},{6,4},{8,10},{10,8},{12,14},{14,12},{1,3},{3,1},... | collective-permute-start | bytes 393224 | tf_op jit(solution)/shard_map/ppermute | solution.py:597
  44.8 5.4 %collective-permute-start.5 = (bf16[4,128,128]{2,1,0:T(8,128)(2,1)S(1)}, bf16[4,128,128]{2,1,0:T(8,128)(2,1)S(1)}, u32[]{:S(2)}, u32[]{:S(2)}) collective-permute-start(bf16[4,128,128]{2,1,0:T(8,128)(2,1)S(1)} %get-tuple-element.65), channel_id=1, source_target_pairs={{0,4},{2,6},{4,0},{6,2},{8,12},{10,14},{12,8},{14,10},{1,5},{3,7},... | collective-permute-start | bytes 393224 | tf_op jit(solution)/shard_map/ppermute | solution.py:597
  45.9 5.9 %collective-permute-start.6 = (bf16[4,128,128]{2,1,0:T(8,128)(2,1)S(1)}, bf16[4,128,128]{2,1,0:T(8,128)(2,1)S(1)}, u32[]{:S(2)}, u32[]{:S(2)}) collective-permute-start(bf16[4,128,128]{2,1,0:T(8,128)(2,1)S(1)} %get-tuple-element.66), channel_id=1, source_target_pairs={{0,6},{2,4},{4,2},{6,0},{8,14},{10,12},{12,10},{14,8},{1,7},{3,5},... | collective-permute-start | bytes 393224 | tf_op jit(solution)/shard_map/ppermute | solution.py:597
  49.5 8.7 %copy-start.4 = (bf16[4,128,128]{2,1,0:T(8,128)(2,1)}, bf16[4,128,128]{2,1,0:T(8,128)(2,1)S(1)}, u32[]{:S(2)}) copy-start(bf16[4,128,128]{2,1,0:T(8,128)(2,1)S(1)} %collective-permute-done.4.e1) | copy-start | bytes 393220
  50.3 7.9 %copy-start.5 = (bf16[4,128,128]{2,1,0:T(8,128)(2,1)}, bf16[4,128,128]{2,1,0:T(8,128)(2,1)S(1)}, u32[]{:S(2)}) copy-start(bf16[4,128,128]{2,1,0:T(8,128)(2,1)S(1)} %collective-permute-done.5.e2) | copy-start | bytes 393220
  51.8 6.4 %copy-start.6 = (bf16[4,128,128]{2,1,0:T(8,128)(2,1)}, bf16[4,128,128]{2,1,0:T(8,128)(2,1)S(1)}, u32[]{:S(2)}) copy-start(bf16[4,128,128]{2,1,0:T(8,128)(2,1)S(1)} %collective-permute-done.6.e3) | copy-start | bytes 393220
  51.8 29.0 %all-to-all-start.2 = ((bf16[8,4,128,128]{3,2,1,0:T(8,128)(2,1)}), bf16[8,4,128,128]{3,2,1,0:T(8,128)(2,1)S(1)}, u32[]{:S(2)}, u32[]{:S(2)}) async-start(bf16[8,4,128,128]{3,2,1,0:T(8,128)(2,1)} %final_states.1), calls=%async_computation.2 | async-start | bytes 2097152 | tf_op jit(solution)/shard_map/all_to_all | solution.py:592

commit v3 on v2

--- a/solution.py
+++ b/solution.py
@@ -128,7 +128,7 @@
             device = (ends[d] - 1) // rows
             rank = jnp.where(device == previous, rank + 1, 0)
             previous = device
-            late = ((rank >= SIDE) & (ends[d] != (device + 1) * rows)).astype(jnp.int32)
+            late = ((rank >= SIDE) & (ends[d] != (device + 1) * rows)).astype(jnp.int32) + (rank > SIDE).astype(jnp.int32)
             crowded = jnp.maximum(crowded, late)
             owned_in = jnp.where(own_ref[d] == me, device, owned_in)
         at = iota((heads, rows), 1)
@@ -610,15 +610,18 @@
     side, crow, flags, *last = piece_states(doc_lengths, owner_ids, decay_rows, keys, values, SIDE)
     last = by_distance(last, spread)
     gain = gain.reshape(1, -1)
-    crowded = flags[1] > 0
     from_quad = [flags[0] == q for q in range(1, quads)]
     slots = max(doc_lengths.shape[0] - 1, SIDE + 1)
 
-    def send_rest():
-        return swap(piece_states(doc_lengths, owner_ids, decay_rows, keys, values, slots)[0], near)
-
-    none = jnp.zeros((MEMBERS, (slots - SIDE) * hp * 128, 128), BF16)
-    rest = lax.cond(crowded, send_rest, lambda: none)
+    def none(count):
+        return jnp.zeros((MEMBERS, count * hp * 128, 128), BF16)
+
+    def send_rest(count):
+        sent = swap(piece_states(doc_lengths, owner_ids, decay_rows, keys, values, count)[0], near)
+        return jnp.concatenate([sent, none(slots - count)], axis=1) if count < slots else sent
+
+    branches = [lambda: none(slots - SIDE), lambda: send_rest(SIDE + 1), lambda: send_rest(slots)]
+    rest = lax.switch(flags[1], branches)
     last, side, gain, rest, from_quad = barrier((last, side, gain, rest, from_quad))
 
     side = swap(side, near)

time: 82.2 us -> 82.4 us (level)
  waiting for transfers between devices: 16.1 us -> 14.7 us
  local copies, waits for them, and re-layouts: 2.29 us -> 3.57 us
    another operation x0 -> x1, local copies, waits for them, and re-layouts: none -> 1.63 us
    ppermute x6, waiting for transfers between devices: 5.66 us -> 4.48 us  [by_distance(): lax.ppermute(parcels[x], 'seq', [(s, s ^ x) for s in range(spread)])]
  transfers between devices with their start and end apart: 9 -> 9, of which waited for: 7 -> 7; matrix products, arithmetic and copies ran while one was open for 3% -> 4% of each run, Pallas kernels for 35% -> 35%
where the time goes in v3:
time: 82.4 us; the launch traced here: 81.7 us
  Pallas kernels  37.5 us (46%)
  starting transfers between devices  23.1 us (28%)
  waiting for transfers between devices  14.7 us (18%)
  local copies, waits for them, and re-layouts  3.57 us (4%)
  between operations  1.97 us (2%)
  other arithmetic  0.85 us (1%)
    pallas_call x1, Pallas kernels, finish(): pl.pallas_call(finish_kernel, grid=(heads // 2,), in_specs=[SMEM, wide, l...  17.7 us
    all_to_all x2, starting transfers between devices, swap(): lax.all_to_all(x, 'seq', split_axis=0, concat_axis=0, axis_index_groups=g...  10.4 us
    ppermute x6, starting transfers between devices, by_distance(): lax.ppermute(parcels[x], 'seq', [(s, s ^ x) for s in range(spread)])  8.13 us
    pallas_call x1, Pallas kernels, early_attention(): pl.pallas_call(functools.partial(early_kernel, skip), grid=(count // 2,),...  8.1 us
    pallas_call x1, Pallas kernels, piece_states(): pl.pallas_call(functools.partial(pieces_kernel, rest), grid=(MEMBERS,), i...  8.03 us
    ppermute x1, waiting for transfers between devices, on_device(): coming = [lax.ppermute(leaving, 'seq', onward)]  5.37 us
    all_to_all x2, waiting for transfers between devices, swap(): lax.all_to_all(x, 'seq', split_axis=0, concat_axis=0, axis_index_groups=g...  4.89 us
    ppermute x1, starting transfers between devices, on_device(): coming = [lax.ppermute(leaving, 'seq', onward)]  4.55 us
  transfers between devices with their start and end apart: 9, of which 7 were waited for; matrix products, arithmetic and copies ran while one was open for 4% of the time, Pallas kernels for 35%

profile of v3, /device:TPU:0, one launch (start us, length us, event | category | flops | bytes accessed | tf_op | source)
XLA Modules:
  0.0 81.7 jit_solution(11936462153647233456)
XLA Ops:
  0.6 0.0 copy-start.8
  0.6 0.0 copy-start.2
  0.7 0.0 copy-start.6
  0.7 0.0 copy-start.7
  0.7 8.0 %piece_states.5 = (bf16[4,1536,128]{2,1,0:T(8,128)(2,1)}, f32[16,1024]{1,0:T(8,128)}, s32[2]{0:T(128)}, bf16[528,128]{1,0:T(8,128)(2,1)}, bf16[528,128]{1,0:T(8,...) custom-call(s32[8]{0:T(128)} %len_ref.11, s32[8]{0:T(128)} %own_ref.3, f32[16,1024]{1,0:T(8,128)} %bitcast.4, ...), custom_call_target="tpu_custom_call" | custom-call | flops 1073741824 | bytes 8388608 | tf_op jit(solution)/shard_map/piece_states/pallas_call | solution.py:235
  8.7 3.0 %collective-permute-start = (bf16[528,128]{1,0:T(8,128)(2,1)}, bf16[528,128]{1,0:T(8,128)(2,1)S(1)}, u32[]{:S(2)}, u32[]{:S(2)}) collective-permute-start(bf16[528,128]{1,0:T(8,128)(2,1)} %get-tuple-element.67), channel_id=1, source_target_pairs={{0,2},{2,0},{4,6},{6,4},{8,10},{10,8},{12,14},{14,12},{1,3},{3,1},... | collective-permute-start | bytes 405512 | tf_op jit(solution)/shard_map/ppermute | solution.py:597
  11.7 1.6 %collective-permute-start.1 = (bf16[528,128]{1,0:T(8,128)(2,1)}, bf16[528,128]{1,0:T(8,128)(2,1)S(1)}, u32[]{:S(2)}, u32[]{:S(2)}) collective-permute-start(bf16[528,128]{1,0:T(8,128)(2,1)} %get-tuple-element.68), channel_id=1, source_target_pairs={{0,4},{2,6},{4,0},{6,2},{8,12},{10,14},{12,8},{14,10},{1,5},{3,7},... | collective-permute-start | bytes 405512 | tf_op jit(solution)/shard_map/ppermute | solution.py:597
  13.3 0.0 collective-permute-start.2
  13.3 0.0 copy-done.8
  13.3 0.6 reshape.39.gain_ref
  13.9 1.3 %fusion = (s32[1]{0:T(128)}, s32[1]{0:T(128)}) fusion(s32[2]{0:T(128)} %get-tuple-element.71), kind=kLoop, calls=%fused_computation.1 | loop fusion | bytes 16 | tf_op jit(solution)/shard_map/slice | solution.py:613
  16.4 0.0 copy-done.2
  16.4 0.0 copy-done.6
  16.4 0.0 copy-done.7
  16.4 1.6 %conditional.1 = (bf16[4,2048,128]{2,1,0:T(8,128)(2,1)}) conditional(s32[]{:T(128)} %bitcast.1, () %tuple.21, (s32[8]{0:T(128)S(1)}, s32[8]{0:T(128)S(1)}, f32[16,1024]{1,0:T(8,128)S(1)}, bf16[1024,2048]{1,0:T(8,128)(2,1)}, bf16[1024,2048]{1,0:T(8,128)(2,1)}) %tuple.36, (s32[8]{0:T(128)S(1)}, s32[8]{0:T(128)S(1)}, ...), branch_computations={%region_0.0_spmd, %region_1.0_spmd, %region_2.0_spmd} | conditional | flops 1073741824 | bytes 12582920 | solution.py:624
  16.4 1.6 %broadcast.13 = bf16[4,2048,128]{2,1,0:T(8,128)(2,1)} broadcast(bf16[]{:T(256)} %constant.3.clone), dimensions={} | broadcast | bytes 2097154 | tf_op jit(solution)/shard_map/broadcast.1
  18.1 0.0 copy-start
  18.1 0.0 collective-permute-done.refs_1_
  18.1 0.3 collective-permute-done.1.refs_2_
  18.4 1.2 %collective-permute-done.2.refs_3_ = bf16[528,128]{1,0:T(8,128)(2,1)S(1)} collective-permute-done((bf16[528,128]{1,0:T(8,128)(2,1)}, bf16[528,128]{1,0:T(8,128)(2,1)S(1)}, u32[]{:S(2)}, u32[]{:S(2)}) %collective-permute-start.2) | collective-permute-done | bytes 135200 | tf_op jit(solution)/shard_map/ppermute | solution.py:597
  19.6 4.0 %all-to-all-start.2 = ((bf16[4,1536,128]{2,1,0:T(8,128)(2,1)}), bf16[4,1536,128]{2,1,0:T(8,128)(2,1)S(1)}, u32[]{:S(2)}, u32[]{:S(2)}) async-start(bf16[4,1536,128]{2,1,0:T(8,128)(2,1)} %get-tuple-element.78), calls=%async_computation.2 | async-start | bytes 3145728 | tf_op jit(solution)/shard_map/all_to_all | solution.py:592
  23.6 0.0 copy-done
  23.6 0.7 leave_quad.1
  24.3 4.6 %collective-permute-start.3 = (bf16[4,128,128]{2,1,0:T(8,128)(2,1)S(1)}, bf16[4,128,128]{2,1,0:T(8,128)(2,1)S(1)}, u32[]{:S(2)}, u32[]{:S(2)}) collective-permute-start(bf16[4,128,128]{2,1,0:T(8,128)(2,1)S(1)} %leave_quad.1), channel_id=1, source_target_pairs={{0,8},{2,10},{4,12},{6,14},{1,9},{3,11},{5,13},{7,15},{16,24},{18,... | collective-permute-start | bytes 393224 | tf_op jit(solution)/shard_map/ppermute | solution.py:631
  28.9 8.1 %early_attention.1.local_ref = f32[1024,1024]{1,0:T(8,128)} custom-call(s32[8]{0:T(128)S(1)} %copy-done.6, bf16[1024,2048]{1,0:T(8,128)(2,1)} %q_ref.3, bf16[1024,2048]{1,0:T(8,128)(2,1)} %k_ref.5, bf16[1024,2048]{1,0:T(8,128)(2,1)} %v_ref.5, f32[16,1024]{1,0:T(8,128)} %get-tuple-element.77.crow_ref), custom_call_target="tpu_custom_call" | custom-call | flops 2147483648 | bytes 10485760 | tf_op jit(solution)/shard_map/early_attention/pallas_call | solution.py:358
  37.0 5.4 %collective-permute-done.3.refs_4_.refs_6_ = bf16[4,128,128]{2,1,0:T(8,128)(2,1)S(1)} collective-permute-done((bf16[4,128,128]{2,1,0:T(8,128)(2,1)S(1)}, bf16[4,128,128]{2,1,0:T(8,128)(2,1)S(1)}, u32[]{:S(2)}, u32[]{:S(2)}) %collective-permute-start.3) | collective-permute-done | bytes 131104 | tf_op jit(solution)/shard_map/ppermute | solution.py:631
  42.4 0.0 all-to-all-done.2.refs_4_
  42.4 0.8 enter_states.1
  43.1 0.0 copy-start.1
  43.1 1.8 %collective-permute-start.4 = (bf16[4,128,128]{2,1,0:T(8,128)(2,1)S(1)}, bf16[4,128,128]{2,1,0:T(8,128)(2,1)S(1)}, u32[]{:S(2)}, u32[]{:S(2)}) collective-permute-start(bf16[4,128,128]{2,1,0:T(8,128)(2,1)S(1)} %get-tuple-element.81), channel_id=1, source_target_pairs={{0,2},{2,0},{4,6},{6,4},{8,10},{10,8},{12,14},{14,12},{1,3},{3,1},... | collective-permute-start | bytes 393224 | tf_op jit(solution)/shard_map/ppermute | solution.py:597
  44.9 1.1 %collective-permute-start.5 = (bf16[4,128,128]{2,1,0:T(8,128)(2,1)S(1)}, bf16[4,128,128]{2,1,0:T(8,128)(2,1)S(1)}, u32[]{:S(2)}, u32[]{:S(2)}) collective-permute-start(bf16[4,128,128]{2,1,0:T(8,128)(2,1)S(1)} %get-tuple-element.82), channel_id=1, source_target_pairs={{0,4},{2,6},{4,0},{6,2},{8,12},{10,14},{12,8},{14,10},{1,5},{3,7},... | collective-permute-start | bytes 393224 | tf_op jit(solution)/shard_map/ppermute | solution.py:597
  46.0 0.7 collective-permute-start.6
  46.7 2.2 %final_states.1 = bf16[8,4,128,128]{3,2,1,0:T(8,128)(2,1)} custom-call(s32[8]{0:T(128)S(1)} %copy-done.6, s32[8]{0:T(128)S(1)} %copy-done.7, bf16[528,128]{1,0:T(8,128)(2,1)S(1)} %copy-done, bf16[528,128]{1,0:T(8,128)(2,1)S(1)} %collective-permute-done.refs_1_, bf16[528,128]{1,0:T(8,128)(2,1)S(1)} %collective-permute-done.1.refs_2_, ...), custom_call_target="tpu_custom_call" | custom-call | tf_op jit(solution)/shard_map/final_states/pallas_call | solution.py:501
  48.9 0.0 copy-done.1
  48.9 0.6 collective-permute-done.4.e1
  49.6 0.0 copy-start.3
  49.6 0.8 collective-permute-done.5.e2
  50.3 0.0 copy-start.4
  50.3 1.5 %collective-permute-done.6.e3 = bf16[4,128,128]{2,1,0:T(8,128)(2,1)S(1)} collective-permute-done((bf16[4,128,128]{2,1,0:T(8,128)(2,1)S(1)}, bf16[4,128,128]{2,1,0:T(8,128)(2,1)S(1)}, u32[]{:S(2)}, u32[]{:S(2)}) %collective-permute-start.6) | collective-permute-done | bytes 131104 | tf_op jit(solution)/shard_map/ppermute | solution.py:597
  51.9 0.0 copy-start.5
  51.9 6.4 %all-to-all-start.3 = ((bf16[8,4,128,128]{3,2,1,0:T(8,128)(2,1)}), bf16[8,4,128,128]{3,2,1,0:T(8,128)(2,1)S(1)}, u32[]{:S(2)}, u32[]{:S(2)}) async-start(bf16[8,4,128,128]{3,2,1,0:T(8,128)(2,1)} %final_states.1), calls=%async_computation.3 | async-start | bytes 2097152 | tf_op jit(solution)/shard_map/all_to_all | solution.py:592
  58.3 0.0 copy-done.3
  58.3 0.0 copy-done.4
  58.3 0.0 copy-done.5
  58.3 17.7 %finish.1 = bf16[1024,2048]{1,0:T(8,128)(2,1)} custom-call(s32[8]{0:T(128)S(1)} %copy-done.6, bf16[1024,2048]{1,0:T(8,128)(2,1)} %q_ref.3, bf16[1024,2048]{1,0:T(8,128)(2,1)} %k_ref.5, bf16[1024,2048]{1,0:T(8,128)(2,1)} %v_ref.5, bf16[4,128,128]{2,1,0:T(8,128)(2,1)} %copy-done.1, bf16[4,128,128]{2,1,0:T(8,128)(2,1)} %copy-done.3, ...), custom_call_target="tpu_custom_call" | custom-call | flops 4294967296 | bytes 20971520 | tf_op jit(solution)/shard_map/finish/pallas_call | solution.py:569
  76.0 4.9 %all-to-all-done.3 = bf16[8,4,128,128]{3,2,1,0:T(8,128)(2,1)S(1)} async-done(((bf16[8,4,128,128]{3,2,1,0:T(8,128)(2,1)}), bf16[8,4,128,128]{3,2,1,0:T(8,128)(2,1)S(1)}, u32[]{:S(2)}, u32[]{:S(2)}) %all-to-all-start.3) | async-done | bytes 1048608 | tf_op jit(solution)/shard_map/all_to_all | solution.py:592
  80.9 0.8 %slice_select_fusion = bf16[4,4,128,128]{3,2,1,0:T(8,128)(2,1)} fusion(bf16[8,4,128,128]{3,2,1,0:T(8,128)(2,1)S(1)} %all-to-all-done.3, pred[]{:T(512)} %bitcast.2), kind=kLoop, calls=%fused_computation | loop fusion | flops 262144 | bytes 1572865 | tf_op jit(solution)/shard_map/jit(_where)/select_n | solution.py:643
Async XLA Ops:
  0.6 12.7 %copy-start.8 = (bf16[2048]{0:T(1024)(128)(2,1)S(1)}, bf16[2048]{0:T(1024)(128)(2,1)}, u32[]{:S(2)}) copy-start(bf16[2048]{0:T(1024)(128)(2,1)} %param.16) | copy-start | bytes 12292
  0.6 15.8 %copy-start.2 = (f32[1024,16]{0,1:T(8,128)S(1)}, f32[1024,16]{0,1:T(8,128)}, u32[]{:S(2)}) copy-start(f32[1024,16]{0,1:T(8,128)} %param.14) | copy-start | bytes 196612
  0.7 15.8 %copy-start.6 = (s32[8]{0:T(128)S(1)}, s32[8]{0:T(128)}, u32[]{:S(2)}) copy-start(s32[8]{0:T(128)} %len_ref.11) | copy-start | bytes 100
  0.7 15.8 %copy-start.7 = (s32[8]{0:T(128)S(1)}, s32[8]{0:T(128)}, u32[]{:S(2)}) copy-start(s32[8]{0:T(128)} %own_ref.3) | copy-start | bytes 100
  8.7 9.4 %collective-permute-start = (bf16[528,128]{1,0:T(8,128)(2,1)}, bf16[528,128]{1,0:T(8,128)(2,1)S(1)}, u32[]{:S(2)}, u32[]{:S(2)}) collective-permute-start(bf16[528,128]{1,0:T(8,128)(2,1)} %get-tuple-element.67), channel_id=1, source_target_pairs={{0,2},{2,0},{4,6},{6,4},{8,10},{10,8},{12,14},{14,12},{1,3},{3,1},... | collective-permute-start | bytes 405512 | tf_op jit(solution)/shard_map/ppermute | solution.py:597
  11.7 6.7 %collective-permute-start.1 = (bf16[528,128]{1,0:T(8,128)(2,1)}, bf16[528,128]{1,0:T(8,128)(2,1)S(1)}, u32[]{:S(2)}, u32[]{:S(2)}) collective-permute-start(bf16[528,128]{1,0:T(8,128)(2,1)} %get-tuple-element.68), channel_id=1, source_target_pairs={{0,4},{2,6},{4,0},{6,2},{8,12},{10,14},{12,8},{14,10},{1,5},{3,7},... | collective-permute-start | bytes 405512 | tf_op jit(solution)/shard_map/ppermute | solution.py:597
  13.3 6.4 %collective-permute-start.2 = (bf16[528,128]{1,0:T(8,128)(2,1)}, bf16[528,128]{1,0:T(8,128)(2,1)S(1)}, u32[]{:S(2)}, u32[]{:S(2)}) collective-permute-start(bf16[528,128]{1,0:T(8,128)(2,1)} %get-tuple-element.69), channel_id=1, source_target_pairs={{0,6},{2,4},{4,2},{6,0},{8,14},{10,12},{12,10},{14,8},{1,7},{3,5},... | collective-permute-start | bytes 405512 | tf_op jit(solution)/shard_map/ppermute | solution.py:597
  18.1 5.5 %copy-start = (bf16[528,128]{1,0:T(8,128)(2,1)S(1)}, bf16[528,128]{1,0:T(8,128)(2,1)}, u32[]{:S(2)}) copy-start(bf16[528,128]{1,0:T(8,128)(2,1)} %get-tuple-element.72.refs_0_) | copy-start | bytes 405508
  19.6 22.7 %all-to-all-start.2 = ((bf16[4,1536,128]{2,1,0:T(8,128)(2,1)}), bf16[4,1536,128]{2,1,0:T(8,128)(2,1)S(1)}, u32[]{:S(2)}, u32[]{:S(2)}) async-start(bf16[4,1536,128]{2,1,0:T(8,128)(2,1)} %get-tuple-element.78), calls=%async_computation.2 | async-start | bytes 3145728 | tf_op jit(solution)/shard_map/all_to_all | solution.py:592
  24.3 18.0 %collective-permute-start.3 = (bf16[4,128,128]{2,1,0:T(8,128)(2,1)S(1)}, bf16[4,128,128]{2,1,0:T(8,128)(2,1)S(1)}, u32[]{:S(2)}, u32[]{:S(2)}) collective-permute-start(bf16[4,128,128]{2,1,0:T(8,128)(2,1)S(1)} %leave_quad.1), channel_id=1, source_target_pairs={{0,8},{2,10},{4,12},{6,14},{1,9},{3,11},{5,13},{7,15},{16,24},{18,... | collective-permute-start | bytes 393224 | tf_op jit(solution)/shard_map/ppermute | solution.py:631
  43.1 5.8 %copy-start.1 = (bf16[4,128,128]{2,1,0:T(8,128)(2,1)}, bf16[4,128,128]{2,1,0:T(8,128)(2,1)S(1)}, u32[]{:S(2)}) copy-start(bf16[4,128,128]{2,1,0:T(8,128)(2,1)S(1)} %get-tuple-element.86.e0) | copy-start | bytes 393220
  43.1 6.4 %collective-permute-start.4 = (bf16[4,128,128]{2,1,0:T(8,128)(2,1)S(1)}, bf16[4,128,128]{2,1,0:T(8,128)(2,1)S(1)}, u32[]{:S(2)}, u32[]{:S(2)}) collective-permute-start(bf16[4,128,128]{2,1,0:T(8,128)(2,1)S(1)} %get-tuple-element.81), channel_id=1, source_target_pairs={{0,2},{2,0},{4,6},{6,4},{8,10},{10,8},{12,14},{14,12},{1,3},{3,1},... | collective-permute-start | bytes 393224 | tf_op jit(solution)/shard_map/ppermute | solution.py:597
  44.9 5.4 %collective-permute-start.5 = (bf16[4,128,128]{2,1,0:T(8,128)(2,1)S(1)}, bf16[4,128,128]{2,1,0:T(8,128)(2,1)S(1)}, u32[]{:S(2)}, u32[]{:S(2)}) collective-permute-start(bf16[4,128,128]{2,1,0:T(8,128)(2,1)S(1)} %get-tuple-element.82), channel_id=1, source_target_pairs={{0,4},{2,6},{4,0},{6,2},{8,12},{10,14},{12,8},{14,10},{1,5},{3,7},... | collective-permute-start | bytes 393224 | tf_op jit(solution)/shard_map/ppermute | solution.py:597
  46.0 5.9 %collective-permute-start.6 = (bf16[4,128,128]{2,1,0:T(8,128)(2,1)S(1)}, bf16[4,128,128]{2,1,0:T(8,128)(2,1)S(1)}, u32[]{:S(2)}, u32[]{:S(2)}) collective-permute-start(bf16[4,128,128]{2,1,0:T(8,128)(2,1)S(1)} %get-tuple-element.83), channel_id=1, source_target_pairs={{0,6},{2,4},{4,2},{6,0},{8,14},{10,12},{12,10},{14,8},{1,7},{3,5},... | collective-permute-start | bytes 393224 | tf_op jit(solution)/shard_map/ppermute | solution.py:597
  49.6 8.7 %copy-start.3 = (bf16[4,128,128]{2,1,0:T(8,128)(2,1)}, bf16[4,128,128]{2,1,0:T(8,128)(2,1)S(1)}, u32[]{:S(2)}) copy-start(bf16[4,128,128]{2,1,0:T(8,128)(2,1)S(1)} %collective-permute-done.4.e1) | copy-start | bytes 393220
  50.3 8.0 %copy-start.4 = (bf16[4,128,128]{2,1,0:T(8,128)(2,1)}, bf16[4,128,128]{2,1,0:T(8,128)(2,1)S(1)}, u32[]{:S(2)}) copy-start(bf16[4,128,128]{2,1,0:T(8,128)(2,1)S(1)} %collective-permute-done.5.e2) | copy-start | bytes 393220
  51.9 6.5 %copy-start.5 = (bf16[4,128,128]{2,1,0:T(8,128)(2,1)}, bf16[4,128,128]{2,1,0:T(8,128)(2,1)S(1)}, u32[]{:S(2)}) copy-start(bf16[4,128,128]{2,1,0:T(8,128)(2,1)S(1)} %collective-permute-done.6.e3) | copy-start | bytes 393220
  51.9 29.0 %all-to-all-start.3 = ((bf16[8,4,128,128]{3,2,1,0:T(8,128)(2,1)}), bf16[8,4,128,128]{3,2,1,0:T(8,128)(2,1)S(1)}, u32[]{:S(2)}, u32[]{:S(2)}) async-start(bf16[8,4,128,128]{3,2,1,0:T(8,128)(2,1)} %final_states.1), calls=%async_computation.3 | async-start | bytes 2097152 | tf_op jit(solution)/shard_map/all_to_all | solution.py:592

commit v4 on v3

--- a/solution.py
+++ b/solution.py
@@ -97,10 +97,10 @@
         side_ref, crow_ref, w_ref, keep_ref = refs
         slots = keep_ref.shape[0]
     else:
-        side_ref, crow_ref, flag_ref = refs[:3]
-        last_refs = refs[3 : 3 + MEMBERS]
-        w_ref, first_ref, high_ref, weighted_ref, prefix_ref = refs[3 + MEMBERS :]
-        slots = SIDE
+        side_ref, crow_ref, flag_ref, spare_ref = refs[:4]
+        last_refs = refs[4 : 4 + MEMBERS]
+        w_ref, first_ref, high_ref, weighted_ref, prefix_ref = refs[4 + MEMBERS :]
+        slots = SIDE + 1
     heads, rows = crow_ref.shape
     step = pl.program_id(0)
     hp = v_ref.shape[1] // 128
@@ -193,8 +193,8 @@
             states = dot(kept.reshape(256, TILE), v_ref[pl.ds(start, TILE), lanes[i]])
             for j in range(2):
                 until = own(states, j) + prefix_ref[tile, i + j]
-                at = (s * hp + i + j) * 128
-                side_ref[0, at : at + 128, :] = (until - ended[i][j]).astype(BF16)
+                out_ref, at = (side_ref, (s * hp + i + j) * 128) if s < SIDE else (spare_ref, (i + j) * 128)
+                out_ref[0, at : at + 128, :] = (until - ended[i][j]).astype(BF16)
                 ended[i][j] = until
     rate = first_ref[pl.ds(step * hp, hp), :]
     high = rate.astype(BF16).astype(F32)
@@ -224,11 +224,13 @@
         scratch.append(pltpu.VMEM((count, 16, rows), BF16))
     else:
         last = (hp * 128 + EXTRA, 128)
-        shapes += [jax.ShapeDtypeStruct((2,), jnp.int32)] + [jax.ShapeDtypeStruct(last, BF16)] * MEMBERS
-        specs += [SMEM] + [whole(last)] * MEMBERS
+        spare = (hp * 128, 128)
+        shapes += [jax.ShapeDtypeStruct((2,), jnp.int32), jax.ShapeDtypeStruct((MEMBERS,) + spare, BF16)]
+        shapes += [jax.ShapeDtypeStruct(last, BF16)] * MEMBERS
+        specs += [SMEM, pl.BlockSpec((1,) + spare, lambda j: (j, 0, 0))] + [whole(last)] * MEMBERS
         scratch += [
             pltpu.VMEM((heads, 128), F32),
-            pltpu.SMEM((SIDE,), jnp.int32),
+            pltpu.SMEM((SIDE + 1,), jnp.int32),
             pltpu.VMEM((hp * 128, rows), BF16),
             pltpu.VMEM((rows // TILE, hp, 128, 128), F32),
         ]
@@ -607,7 +609,7 @@
     decay_rows = log_decay.T
     barrier = lax.optimization_barrier
 
-    side, crow, flags, *last = piece_states(doc_lengths, owner_ids, decay_rows, keys, values, SIDE)
+    side, crow, flags, spare, *last = piece_states(doc_lengths, owner_ids, decay_rows, keys, values, SIDE)
     last = by_distance(last, spread)
     gain = gain.reshape(1, -1)
     from_quad = [flags[0] == q for q in range(1, quads)]
@@ -616,11 +618,13 @@
     def none(count):
         return jnp.zeros((MEMBERS, count * hp * 128, 128), BF16)
 
-    def send_rest(count):
-        sent = swap(piece_states(doc_lengths, owner_ids, decay_rows, keys, values, count)[0], near)
-        return jnp.concatenate([sent, none(slots - count)], axis=1) if count < slots else sent
-
-    branches = [lambda: none(slots - SIDE), lambda: send_rest(SIDE + 1), lambda: send_rest(slots)]
+    def send_one():
+        return jnp.concatenate([swap(spare, near), none(slots - SIDE - 1)], axis=1)
+
+    def send_rest():
+        return swap(piece_states(doc_lengths, owner_ids, decay_rows, keys, values, slots)[0], near)
+
+    branches = [lambda: none(slots - SIDE), send_one, send_rest]
     rest = lax.switch(flags[1], branches)
     last, side, gain, rest, from_quad = barrier((last, side, gain, rest, from_quad))
 

time: 82.4 us -> 82.6 us (level)
  no operation moved by 1% of the time
where the time goes in v4:
time: 82.6 us; the launch traced here: 82.1 us
  Pallas kernels  37.8 us (46%)
  starting transfers between devices  22.8 us (28%)
  waiting for transfers between devices  15 us (18%)
  local copies, waits for them, and re-layouts  3.63 us (4%)
  between operations  1.94 us (2%)
  other arithmetic  0.85 us (1%)
    pallas_call x1, Pallas kernels, finish(): pl.pallas_call(finish_kernel, grid=(heads // 2,), in_specs=[SMEM, wide, l...  17.7 us
    all_to_all x2, starting transfers between devices, swap(): lax.all_to_all(x, 'seq', split_axis=0, concat_axis=0, axis_index_groups=g...  10.2 us
    pallas_call x1, Pallas kernels, piece_states(): pl.pallas_call(functools.partial(pieces_kernel, rest), grid=(MEMBERS,), i...  8.29 us
    ppermute x6, starting transfers between devices, by_distance(): lax.ppermute(parcels[x], 'seq', [(s, s ^ x) for s in range(spread)])  8.12 us
    pallas_call x1, Pallas kernels, early_attention(): pl.pallas_call(functools.partial(early_kernel, skip), grid=(count // 2,),...  8.11 us
    ppermute x1, waiting for transfers between devices, on_device(): coming = [lax.ppermute(leaving, 'seq', onward)]  5.53 us
    all_to_all x2, waiting for transfers between devices, swap(): lax.all_to_all(x, 'seq', split_axis=0, concat_axis=0, axis_index_groups=g...  4.99 us
    ppermute x1, starting transfers between devices, on_device(): coming = [lax.ppermute(leaving, 'seq', onward)]  4.49 us
  transfers between devices with their start and end apart: 9, of which 7 were waited for; matrix products, arithmetic and copies ran while one was open for 4% of the time, Pallas kernels for 35%

profile of v4, /device:TPU:0, one launch (start us, length us, event | category | flops | bytes accessed | tf_op | source)
XLA Modules:
  0.0 82.1 jit_solution(6249907474012246098)
XLA Ops:
  0.6 0.0 copy-start.8
  0.6 0.0 copy-start.2
  0.7 0.0 copy-start.6
  0.7 0.0 copy-start.7
  0.7 8.3 %piece_states.3 = (bf16[4,1536,128]{2,1,0:T(8,128)(2,1)}, f32[16,1024]{1,0:T(8,128)}, s32[2]{0:T(128)}, bf16[4,512,128]{2,1,0:T(8,128)(2,1)S(1)}, bf16[528,128]{...) custom-call(s32[8]{0:T(128)} %len_ref.11, s32[8]{0:T(128)} %own_ref.3, ...), custom_call_target="tpu_custom_call" | custom-call | flops 1073741824 | bytes 8388608 | tf_op jit(solution)/shard_map/piece_states/pallas_call | solution.py:237
  9.0 3.0 %collective-permute-start = (bf16[528,128]{1,0:T(8,128)(2,1)}, bf16[528,128]{1,0:T(8,128)(2,1)S(1)}, u32[]{:S(2)}, u32[]{:S(2)}) collective-permute-start(bf16[528,128]{1,0:T(8,128)(2,1)} %get-tuple-element.53), channel_id=1, source_target_pairs={{0,2},{2,0},{4,6},{6,4},{8,10},{10,8},{12,14},{14,12},{1,3},{3,1},... | collective-permute-start | bytes 405512 | tf_op jit(solution)/shard_map/ppermute | solution.py:599
  12.0 1.5 %collective-permute-start.1 = (bf16[528,128]{1,0:T(8,128)(2,1)}, bf16[528,128]{1,0:T(8,128)(2,1)S(1)}, u32[]{:S(2)}, u32[]{:S(2)}) collective-permute-start(bf16[528,128]{1,0:T(8,128)(2,1)} %get-tuple-element.54), channel_id=1, source_target_pairs={{0,4},{2,6},{4,0},{6,2},{8,12},{10,14},{12,8},{14,10},{1,5},{3,7},... | collective-permute-start | bytes 405512 | tf_op jit(solution)/shard_map/ppermute | solution.py:599
  13.5 0.0 collective-permute-start.2
  13.5 0.0 copy-done.8
  13.5 0.6 reshape.39.gain_ref
  14.1 1.4 %fusion = (s32[1]{0:T(128)}, s32[1]{0:T(128)}) fusion(s32[2]{0:T(128)} %get-tuple-element.57), kind=kLoop, calls=%fused_computation.1 | loop fusion | bytes 16 | tf_op jit(solution)/shard_map/slice | solution.py:615
  16.7 0.0 copy-done.2
  16.7 0.0 copy-done.6
  16.7 0.0 copy-done.7
  16.7 1.6 %conditional.1 = (bf16[4,2048,128]{2,1,0:T(8,128)(2,1)}) conditional(s32[]{:T(128)} %bitcast.1, () %tuple.21, bf16[4,512,128]{2,1,0:T(8,128)(2,1)S(1)} %get-tuple-element.58, (s32[8]{0:T(128)S(1)}, s32[8]{0:T(128)S(1)}, f32[16,1024]{1,0:T(8,128)S(1)}, bf16[1024,2048]{1,0:T(8,128)(2,1)}, bf16[1024,2048]{1,0:T(8,128)(2,1)}) %tuple.34), branch_computations={%region_0.0_spmd, %region_1.0_spmd, %region_2.0_spmd} | conditional | flops 1073741824 | bytes 12582920 | solution.py:628
  16.7 1.6 %broadcast.13 = bf16[4,2048,128]{2,1,0:T(8,128)(2,1)} broadcast(bf16[]{:T(256)} %constant.3.clone), dimensions={} | broadcast | bytes 2097154 | tf_op jit(solution)/shard_map/broadcast.1
  18.4 0.0 copy-start
  18.4 0.0 collective-permute-done.refs_1_
  18.4 0.3 collective-permute-done.1.refs_2_
  18.7 1.2 %collective-permute-done.2.refs_3_ = bf16[528,128]{1,0:T(8,128)(2,1)S(1)} collective-permute-done((bf16[528,128]{1,0:T(8,128)(2,1)}, bf16[528,128]{1,0:T(8,128)(2,1)S(1)}, u32[]{:S(2)}, u32[]{:S(2)}) %collective-permute-start.2) | collective-permute-done | bytes 135200 | tf_op jit(solution)/shard_map/ppermute | solution.py:599
  19.9 3.9 %all-to-all-start.2 = ((bf16[4,1536,128]{2,1,0:T(8,128)(2,1)}), bf16[4,1536,128]{2,1,0:T(8,128)(2,1)S(1)}, u32[]{:S(2)}, u32[]{:S(2)}) async-start(bf16[4,1536,128]{2,1,0:T(8,128)(2,1)} %get-tuple-element.65), calls=%async_computation.2 | async-start | bytes 3145728 | tf_op jit(solution)/shard_map/all_to_all | solution.py:594
  23.8 0.0 copy-done
  23.8 0.7 leave_quad.1
  24.6 4.5 %collective-permute-start.3 = (bf16[4,128,128]{2,1,0:T(8,128)(2,1)S(1)}, bf16[4,128,128]{2,1,0:T(8,128)(2,1)S(1)}, u32[]{:S(2)}, u32[]{:S(2)}) collective-permute-start(bf16[4,128,128]{2,1,0:T(8,128)(2,1)S(1)} %leave_quad.1), channel_id=1, source_target_pairs={{0,8},{2,10},{4,12},{6,14},{1,9},{3,11},{5,13},{7,15},{16,24},{18,... | collective-permute-start | bytes 393224 | tf_op jit(solution)/shard_map/ppermute | solution.py:635
  29.1 8.1 %early_attention.1.local_ref = f32[1024,1024]{1,0:T(8,128)} custom-call(s32[8]{0:T(128)S(1)} %copy-done.6, bf16[1024,2048]{1,0:T(8,128)(2,1)} %q_ref.3, bf16[1024,2048]{1,0:T(8,128)(2,1)} %k_ref.5, bf16[1024,2048]{1,0:T(8,128)(2,1)} %v_ref.5, f32[16,1024]{1,0:T(8,128)} %get-tuple-element.64.crow_ref), custom_call_target="tpu_custom_call" | custom-call | flops 2147483648 | bytes 10485760 | tf_op jit(solution)/shard_map/early_attention/pallas_call | solution.py:360
  37.2 5.5 %collective-permute-done.3.refs_4_.refs_6_ = bf16[4,128,128]{2,1,0:T(8,128)(2,1)S(1)} collective-permute-done((bf16[4,128,128]{2,1,0:T(8,128)(2,1)S(1)}, bf16[4,128,128]{2,1,0:T(8,128)(2,1)S(1)}, u32[]{:S(2)}, u32[]{:S(2)}) %collective-permute-start.3) | collective-permute-done | bytes 131104 | tf_op jit(solution)/shard_map/ppermute | solution.py:635
  42.7 0.0 all-to-all-done.2.refs_4_
  42.7 0.8 enter_states.1
  43.5 0.0 copy-start.1
  43.5 1.8 %collective-permute-start.4 = (bf16[4,128,128]{2,1,0:T(8,128)(2,1)S(1)}, bf16[4,128,128]{2,1,0:T(8,128)(2,1)S(1)}, u32[]{:S(2)}, u32[]{:S(2)}) collective-permute-start(bf16[4,128,128]{2,1,0:T(8,128)(2,1)S(1)} %get-tuple-element.68), channel_id=1, source_target_pairs={{0,2},{2,0},{4,6},{6,4},{8,10},{10,8},{12,14},{14,12},{1,3},{3,1},... | collective-permute-start | bytes 393224 | tf_op jit(solution)/shard_map/ppermute | solution.py:599
  45.3 1.1 %collective-permute-start.5 = (bf16[4,128,128]{2,1,0:T(8,128)(2,1)S(1)}, bf16[4,128,128]{2,1,0:T(8,128)(2,1)S(1)}, u32[]{:S(2)}, u32[]{:S(2)}) collective-permute-start(bf16[4,128,128]{2,1,0:T(8,128)(2,1)S(1)} %get-tuple-element.69), channel_id=1, source_target_pairs={{0,4},{2,6},{4,0},{6,2},{8,12},{10,14},{12,8},{14,10},{1,5},{3,7},... | collective-permute-start | bytes 393224 | tf_op jit(solution)/shard_map/ppermute | solution.py:599
  46.4 0.7 collective-permute-start.6
  47.0 2.3 %final_states.1 = bf16[8,4,128,128]{3,2,1,0:T(8,128)(2,1)} custom-call(s32[8]{0:T(128)S(1)} %copy-done.6, s32[8]{0:T(128)S(1)} %copy-done.7, bf16[528,128]{1,0:T(8,128)(2,1)S(1)} %copy-done, bf16[528,128]{1,0:T(8,128)(2,1)S(1)} %collective-permute-done.refs_1_, bf16[528,128]{1,0:T(8,128)(2,1)S(1)} %collective-permute-done.1.refs_2_, ...), custom_call_target="tpu_custom_call" | custom-call | tf_op jit(solution)/shard_map/final_states/pallas_call | solution.py:503
  49.3 0.0 copy-done.1
  49.3 0.6 collective-permute-done.4.e1
  49.9 0.0 copy-start.3
  49.9 0.8 collective-permute-done.5.e2
  50.7 0.0 copy-start.4
  50.7 1.5 %collective-permute-done.6.e3 = bf16[4,128,128]{2,1,0:T(8,128)(2,1)S(1)} collective-permute-done((bf16[4,128,128]{2,1,0:T(8,128)(2,1)S(1)}, bf16[4,128,128]{2,1,0:T(8,128)(2,1)S(1)}, u32[]{:S(2)}, u32[]{:S(2)}) %collective-permute-start.6) | collective-permute-done | bytes 131104 | tf_op jit(solution)/shard_map/ppermute | solution.py:599
  52.2 0.0 copy-start.5
  52.2 6.3 %all-to-all-start.3 = ((bf16[8,4,128,128]{3,2,1,0:T(8,128)(2,1)}), bf16[8,4,128,128]{3,2,1,0:T(8,128)(2,1)S(1)}, u32[]{:S(2)}, u32[]{:S(2)}) async-start(bf16[8,4,128,128]{3,2,1,0:T(8,128)(2,1)} %final_states.1), calls=%async_computation.3 | async-start | bytes 2097152 | tf_op jit(solution)/shard_map/all_to_all | solution.py:594
  58.6 0.0 copy-done.3
  58.6 0.0 copy-done.4
  58.6 0.0 copy-done.5
  58.6 17.7 %finish.1 = bf16[1024,2048]{1,0:T(8,128)(2,1)} custom-call(s32[8]{0:T(128)S(1)} %copy-done.6, bf16[1024,2048]{1,0:T(8,128)(2,1)} %q_ref.3, bf16[1024,2048]{1,0:T(8,128)(2,1)} %k_ref.5, bf16[1024,2048]{1,0:T(8,128)(2,1)} %v_ref.5, bf16[4,128,128]{2,1,0:T(8,128)(2,1)} %copy-done.1, bf16[4,128,128]{2,1,0:T(8,128)(2,1)} %copy-done.3, ...), custom_call_target="tpu_custom_call" | custom-call | flops 4294967296 | bytes 20971520 | tf_op jit(solution)/shard_map/finish/pallas_call | solution.py:571
  76.3 5.0 %all-to-all-done.3 = bf16[8,4,128,128]{3,2,1,0:T(8,128)(2,1)S(1)} async-done(((bf16[8,4,128,128]{3,2,1,0:T(8,128)(2,1)}), bf16[8,4,128,128]{3,2,1,0:T(8,128)(2,1)S(1)}, u32[]{:S(2)}, u32[]{:S(2)}) %all-to-all-start.3) | async-done | bytes 1048608 | tf_op jit(solution)/shard_map/all_to_all | solution.py:594
  81.2 0.8 %slice_select_fusion = bf16[4,4,128,128]{3,2,1,0:T(8,128)(2,1)} fusion(bf16[8,4,128,128]{3,2,1,0:T(8,128)(2,1)S(1)} %all-to-all-done.3, pred[]{:T(512)} %bitcast.2), kind=kLoop, calls=%fused_computation | loop fusion | flops 262144 | bytes 1572865 | tf_op jit(solution)/shard_map/jit(_where)/select_n | solution.py:647
Async XLA Ops:
  0.6 12.9 %copy-start.8 = (bf16[2048]{0:T(1024)(128)(2,1)S(1)}, bf16[2048]{0:T(1024)(128)(2,1)}, u32[]{:S(2)}) copy-start(bf16[2048]{0:T(1024)(128)(2,1)} %param.16) | copy-start | bytes 12292
  0.6 16.1 %copy-start.2 = (f32[1024,16]{0,1:T(8,128)S(1)}, f32[1024,16]{0,1:T(8,128)}, u32[]{:S(2)}) copy-start(f32[1024,16]{0,1:T(8,128)} %param.14) | copy-start | bytes 196612
  0.7 16.1 %copy-start.6 = (s32[8]{0:T(128)S(1)}, s32[8]{0:T(128)}, u32[]{:S(2)}) copy-start(s32[8]{0:T(128)} %len_ref.11) | copy-start | bytes 100
  0.7 16.1 %copy-start.7 = (s32[8]{0:T(128)S(1)}, s32[8]{0:T(128)}, u32[]{:S(2)}) copy-start(s32[8]{0:T(128)} %own_ref.3) | copy-start | bytes 100
  9.0 9.4 %collective-permute-start = (bf16[528,128]{1,0:T(8,128)(2,1)}, bf16[528,128]{1,0:T(8,128)(2,1)S(1)}, u32[]{:S(2)}, u32[]{:S(2)}) collective-permute-start(bf16[528,128]{1,0:T(8,128)(2,1)} %get-tuple-element.53), channel_id=1, source_target_pairs={{0,2},{2,0},{4,6},{6,4},{8,10},{10,8},{12,14},{14,12},{1,3},{3,1},... | collective-permute-start | bytes 405512 | tf_op jit(solution)/shard_map/ppermute | solution.py:599
  12.0 6.7 %collective-permute-start.1 = (bf16[528,128]{1,0:T(8,128)(2,1)}, bf16[528,128]{1,0:T(8,128)(2,1)S(1)}, u32[]{:S(2)}, u32[]{:S(2)}) collective-permute-start(bf16[528,128]{1,0:T(8,128)(2,1)} %get-tuple-element.54), channel_id=1, source_target_pairs={{0,4},{2,6},{4,0},{6,2},{8,12},{10,14},{12,8},{14,10},{1,5},{3,7},... | collective-permute-start | bytes 405512 | tf_op jit(solution)/shard_map/ppermute | solution.py:599
  13.5 6.4 %collective-permute-start.2 = (bf16[528,128]{1,0:T(8,128)(2,1)}, bf16[528,128]{1,0:T(8,128)(2,1)S(1)}, u32[]{:S(2)}, u32[]{:S(2)}) collective-permute-start(bf16[528,128]{1,0:T(8,128)(2,1)} %get-tuple-element.55), channel_id=1, source_target_pairs={{0,6},{2,4},{4,2},{6,0},{8,14},{10,12},{12,10},{14,8},{1,7},{3,5},... | collective-permute-start | bytes 405512 | tf_op jit(solution)/shard_map/ppermute | solution.py:599
  18.4 5.5 %copy-start = (bf16[528,128]{1,0:T(8,128)(2,1)S(1)}, bf16[528,128]{1,0:T(8,128)(2,1)}, u32[]{:S(2)}) copy-start(bf16[528,128]{1,0:T(8,128)(2,1)} %get-tuple-element.59.refs_0_) | copy-start | bytes 405508
  19.9 22.8 %all-to-all-start.2 = ((bf16[4,1536,128]{2,1,0:T(8,128)(2,1)}), bf16[4,1536,128]{2,1,0:T(8,128)(2,1)S(1)}, u32[]{:S(2)}, u32[]{:S(2)}) async-start(bf16[4,1536,128]{2,1,0:T(8,128)(2,1)} %get-tuple-element.65), calls=%async_computation.2 | async-start | bytes 3145728 | tf_op jit(solution)/shard_map/all_to_all | solution.py:594
  24.6 18.1 %collective-permute-start.3 = (bf16[4,128,128]{2,1,0:T(8,128)(2,1)S(1)}, bf16[4,128,128]{2,1,0:T(8,128)(2,1)S(1)}, u32[]{:S(2)}, u32[]{:S(2)}) collective-permute-start(bf16[4,128,128]{2,1,0:T(8,128)(2,1)S(1)} %leave_quad.1), channel_id=1, source_target_pairs={{0,8},{2,10},{4,12},{6,14},{1,9},{3,11},{5,13},{7,15},{16,24},{18,... | collective-permute-start | bytes 393224 | tf_op jit(solution)/shard_map/ppermute | solution.py:635
  43.5 5.9 %copy-start.1 = (bf16[4,128,128]{2,1,0:T(8,128)(2,1)}, bf16[4,128,128]{2,1,0:T(8,128)(2,1)S(1)}, u32[]{:S(2)}) copy-start(bf16[4,128,128]{2,1,0:T(8,128)(2,1)S(1)} %get-tuple-element.73.e0) | copy-start | bytes 393220
  43.5 6.4 %collective-permute-start.4 = (bf16[4,128,128]{2,1,0:T(8,128)(2,1)S(1)}, bf16[4,128,128]{2,1,0:T(8,128)(2,1)S(1)}, u32[]{:S(2)}, u32[]{:S(2)}) collective-permute-start(bf16[4,128,128]{2,1,0:T(8,128)(2,1)S(1)} %get-tuple-element.68), channel_id=1, source_target_pairs={{0,2},{2,0},{4,6},{6,4},{8,10},{10,8},{12,14},{14,12},{1,3},{3,1},... | collective-permute-start | bytes 393224 | tf_op jit(solution)/shard_map/ppermute | solution.py:599
  45.3 5.4 %collective-permute-start.5 = (bf16[4,128,128]{2,1,0:T(8,128)(2,1)S(1)}, bf16[4,128,128]{2,1,0:T(8,128)(2,1)S(1)}, u32[]{:S(2)}, u32[]{:S(2)}) collective-permute-start(bf16[4,128,128]{2,1,0:T(8,128)(2,1)S(1)} %get-tuple-element.69), channel_id=1, source_target_pairs={{0,4},{2,6},{4,0},{6,2},{8,12},{10,14},{12,8},{14,10},{1,5},{3,7},... | collective-permute-start | bytes 393224 | tf_op jit(solution)/shard_map/ppermute | solution.py:599
  46.4 5.9 %collective-permute-start.6 = (bf16[4,128,128]{2,1,0:T(8,128)(2,1)S(1)}, bf16[4,128,128]{2,1,0:T(8,128)(2,1)S(1)}, u32[]{:S(2)}, u32[]{:S(2)}) collective-permute-start(bf16[4,128,128]{2,1,0:T(8,128)(2,1)S(1)} %get-tuple-element.70), channel_id=1, source_target_pairs={{0,6},{2,4},{4,2},{6,0},{8,14},{10,12},{12,10},{14,8},{1,7},{3,5},... | collective-permute-start | bytes 393224 | tf_op jit(solution)/shard_map/ppermute | solution.py:599
  49.9 8.6 %copy-start.3 = (bf16[4,128,128]{2,1,0:T(8,128)(2,1)}, bf16[4,128,128]{2,1,0:T(8,128)(2,1)S(1)}, u32[]{:S(2)}) copy-start(bf16[4,128,128]{2,1,0:T(8,128)(2,1)S(1)} %collective-permute-done.4.e1) | copy-start | bytes 393220
  50.7 7.9 %copy-start.4 = (bf16[4,128,128]{2,1,0:T(8,128)(2,1)}, bf16[4,128,128]{2,1,0:T(8,128)(2,1)S(1)}, u32[]{:S(2)}) copy-start(bf16[4,128,128]{2,1,0:T(8,128)(2,1)S(1)} %collective-permute-done.5.e2) | copy-start | bytes 393220
  52.2 6.4 %copy-start.5 = (bf16[4,128,128]{2,1,0:T(8,128)(2,1)}, bf16[4,128,128]{2,1,0:T(8,128)(2,1)S(1)}, u32[]{:S(2)}) copy-start(bf16[4,128,128]{2,1,0:T(8,128)(2,1)S(1)} %collective-permute-done.6.e3) | copy-start | bytes 393220
  52.2 29.0 %all-to-all-start.3 = ((bf16[8,4,128,128]{3,2,1,0:T(8,128)(2,1)}), bf16[8,4,128,128]{3,2,1,0:T(8,128)(2,1)S(1)}, u32[]{:S(2)}, u32[]{:S(2)}) async-start(bf16[8,4,128,128]{3,2,1,0:T(8,128)(2,1)} %final_states.1), calls=%async_computation.3 | async-start | bytes 2097152 | tf_op jit(solution)/shard_map/all_to_all | solution.py:594
